TPU v7x, 32 devices: a whole 2x2x4 slice. The times are simulated.
32 devices in a mesh: dp: 2 (over core), region: 16 (over z, y, x).
Axes of the slice: x: 2, y: 2, z: 4, core: 2. Of those that a mesh axis runs over, the one named last changes fastest.
Arguments:
- cell_counts: int32 [16384], P('dp'), may hold values from 61 to 6144, as said below
- cell_seeds: int32 [16384], P('dp'), may hold values from 0 to 12287
- batch_ids: int32 [16384], P('dp'), may hold values from 0 to 7
- noise_draw: float32 [16384, 10], P('dp'), may hold values from -4 to 4
- cell_factor: float32 [16384], P('dp'), may hold values from 0.3 to 0.95
- enc_weight: float32 [12288, 128], P('region', 'dp'), may hold values from -0.0546875 to 0.0546875
- enc_first: float32 [12288, 128], P('region', 'dp'), may hold values from -1.1444092e-05 to 1.1444092e-05
- enc_second: float32 [12288, 128], P('region', 'dp'), may hold values from 3.4924596e-12 to 1.3969838e-11
- dec_weight: float32 [128, 12288], P('dp', 'region'), may hold values from -0.5 to 0.5
- dec_first: float32 [128, 12288], P('dp', 'region'), may hold values from -7.1525574e-07 to 7.1525574e-07
- dec_second: float32 [128, 12288], P('dp', 'region'), may hold values from 1.6168795e-14 to 6.467518e-14
- region_vecs: float32 [2, 12288], P('dp', 'region')
- vec_first: float32 [2, 12288], P('dp', 'region'), may hold values from -1.335144e-05 to 1.335144e-05
- vec_second: float32 [2, 12288], P('dp', 'region'), may hold values from 4.6566128e-12 to 1.8626451e-11
- trunk_rows: float32 [290, 128], replicated
- trunk_first: float32 [290, 128], replicated, may hold values from -1.5258789e-05 to 1.5258789e-05
- trunk_second: float32 [290, 128], replicated, may hold values from 6.2088173e-12 to 2.483527e-11
- head_rows: float32 [129, 20], replicated
- head_first: float32 [129, 20], replicated, may hold values from -1.5258789e-05 to 1.5258789e-05
- head_second: float32 [129, 20], replicated, may hold values from 6.2088173e-12 to 2.483527e-11
Outputs:
- loss: float32 [2], replicated
- enc_new: float32 [12288, 128], P('region', 'dp')
- enc_first_new: float32 [12288, 128], P('region', 'dp')
- enc_second_new: float32 [12288, 128], P('region', 'dp')
- enc_copy: bfloat16 [12288, 128], P('region', 'dp')
- dec_new: float32 [128, 12288], P('dp', 'region')
- dec_first_new: float32 [128, 12288], P('dp', 'region')
- dec_second_new: float32 [128, 12288], P('dp', 'region')
- dec_copy: bfloat16 [128, 12288], P('dp', 'region')
- vecs_new: float32 [2, 12288], P('dp', 'region')
- vec_first_new: float32 [2, 12288], P('dp', 'region')
- vec_second_new: float32 [2, 12288], P('dp', 'region')
- trunk_new: float32 [290, 128], replicated
- trunk_first_new: float32 [290, 128], replicated
- trunk_second_new: float32 [290, 128], replicated
- head_new: float32 [129, 20], replicated
- head_first_new: float32 [129, 20], replicated
- head_second_new: float32 [129, 20], replicated
- norms: float32 [2, 10], replicated
Inputs may be any that keep to these rules, and one draw needn't show every extreme that they name: Each cell opens exactly cell_counts regions, given by the rule of the first step; some cell holds the smallest and some the largest count.
All inputs are finite; a program needn't handle non-finite values.
Results may differ from a plain program's by a relative error of at most 0.002.
The roundings to bfloat16 on the way count: a program that leaves them out, or rounds other values in their place, can miss the bound.
Values may be sent and summed in bfloat16 or wider, within the bound.
No kernel may reach another device: no remote copies, remote signals or barrier semaphores. Data moves between devices by JAX's collectives and lax.ppermute only.
A program may use at most 128 MiB of HBM per device.

v0:
```python
import jax
import jax.numpy as jnp
from jax import lax
from jax.sharding import PartitionSpec as P

BATCHES = 8


highest = lax.Precision.HIGHEST
norm_eps = 1e-05
leak_slope = 0.01
decay_rate = 0.5
weight_decay = 0.01
learn_rate = 0.5
lamb_eps = 1e-12


def matmul(left, right):
    return jnp.dot(left, right, precision=highest, preferred_element_type=jnp.float32)


def layer_norm(values, gain_row, shift_row):
    centre = values - jnp.mean(values, axis=-1, keepdims=True)
    spread = jnp.mean(centre * centre, axis=-1, keepdims=True)
    return centre * lax.rsqrt(spread + norm_eps) * gain_row + shift_row


def leaky_relu(values):
    return jnp.where(values >= 0, values, leak_slope * values)


def region_masks(counts, seed_rows, first_region, width, total):
    regions = first_region + jnp.arange(width, dtype=jnp.int32)
    stride = 6 * (seed_rows % (total // 6)) + 1
    upper = stride[:, None] * (regions[None, :] // 256) % total
    hashed = (upper * 256 + stride[:, None] * (regions[None, :] % 256) + seed_rows[:, None]) % total
    return hashed < counts[:, None]


def trunk_forward(pre_in, trunk_part, head_part, noise_rows, onehot):
    hidden = trunk_part.shape[1]
    latent = head_part.shape[1] // 2
    batches = onehot.shape[1]
    enc_two = trunk_part[batches : batches + hidden]
    dec_one = trunk_part[batches + hidden : 2 * batches + hidden + latent]
    dec_two = trunk_part[2 * batches + hidden + latent : 2 * batches + 2 * hidden + latent]
    base_row = 2 * batches + 2 * hidden + latent
    gain_rows = trunk_part[base_row : base_row + 4]
    shift_rows = trunk_part[base_row + 4 : base_row + 8]
    first = leaky_relu(layer_norm(pre_in, gain_rows[0], shift_rows[0]))
    second = leaky_relu(layer_norm(matmul(first, enc_two), gain_rows[1], shift_rows[1]))
    moments = matmul(second, head_part[:hidden]) + head_part[hidden]
    centre_lat = moments[:, :latent]
    log_var = moments[:, latent:]
    sample = centre_lat + jnp.exp(0.5 * log_var) * noise_rows
    third_in = matmul(sample, dec_one[:latent]) + matmul(onehot, dec_one[latent:])
    third = leaky_relu(layer_norm(third_in, gain_rows[2], shift_rows[2]))
    fourth = leaky_relu(layer_norm(matmul(third, dec_two), gain_rows[3], shift_rows[3]))
    diverge = 0.5 * jnp.sum(jnp.exp(log_var) + centre_lat * centre_lat - 1.0 - log_var)
    return (fourth, diverge)


def lamb_moments(weight, grad, first, second):
    first_new = decay_rate * first + (1.0 - decay_rate) * grad
    second_new = decay_rate * second + (1.0 - decay_rate) * grad * grad
    update = first_new / (jnp.sqrt(second_new) + lamb_eps) + weight_decay * weight
    return (first_new, second_new, update)


def square_norm(values):
    return jnp.sqrt(jnp.sum(values * values))


def lamb_groups(weight, update, row_edges):
    pieces = []
    weight_list = []
    update_list = []
    for group_index in range(len(row_edges) - 1):
        start_row = row_edges[group_index]
        end_row = row_edges[group_index + 1]
        weight_part = weight[start_row:end_row]
        update_part = update[start_row:end_row]
        weight_norm = square_norm(weight_part)
        update_norm = square_norm(update_part)
        weight_list.append(weight_norm)
        update_list.append(update_norm)
        pieces.append(weight_part - learn_rate * (weight_norm / update_norm) * update_part)
    return (jnp.concatenate(pieces, axis=0), jnp.stack(weight_list), jnp.stack(update_list))


def weight_squares(enc_weight, dec_weight, region_vecs, slot_rows):
    pair = jnp.stack([jnp.sum(enc_weight * enc_weight), jnp.sum(dec_weight * dec_weight)])
    return jnp.concatenate([pair, slot_rows * jnp.sum(region_vecs * region_vecs)])


def on_device(
    cell_counts,
    cell_seeds,
    batch_ids,
    noise_draw,
    cell_factor,
    enc_weight,
    enc_first,
    enc_second,
    dec_weight,
    dec_first,
    dec_second,
    region_vecs,
    vec_first,
    vec_second,
    trunk_rows,
    trunk_first,
    trunk_second,
    head_rows,
    head_first,
    head_second,
):
    cells_here = cell_counts.shape[0]
    regions_here = enc_weight.shape[0]
    hidden = trunk_rows.shape[1]
    latent = head_rows.shape[1] // 2
    region_count = lax.axis_size("region")
    total_regions = regions_here * region_count
    all_cells = cells_here * lax.axis_size("dp")
    loss_scale = 1.0 / (all_cells * total_regions)
    first_region = lax.axis_index("region") * regions_here
    row_index = lax.axis_index("dp")
    slot_rows = (jnp.arange(2, dtype=jnp.int32) == row_index).astype(jnp.float32)
    block_rows = min(1024, cells_here)
    blocks = cells_here // block_rows
    enc_low, dec_low, vec_low = (
        lax.all_gather(enc_weight.astype(jnp.bfloat16), "dp", axis=1, tiled=True),
        lax.all_gather(dec_weight.astype(jnp.bfloat16), "dp", axis=0, tiled=True),
        lax.all_gather(region_vecs.astype(jnp.bfloat16), "dp", axis=0, tiled=True),
    )
    counts_blocks = cell_counts.reshape(blocks, block_rows)
    seed_blocks = cell_seeds.reshape(blocks, block_rows)

    def encode_block(carried, inputs):
        mask_rows = region_masks(
            inputs[0], inputs[1], first_region, regions_here, total_regions
        ).astype(jnp.bfloat16)
        return (carried, jnp.dot(mask_rows, enc_low, preferred_element_type=jnp.float32))

    _, partial_pre = lax.scan(
        encode_block, jnp.zeros((), jnp.float32), (counts_blocks, seed_blocks)
    )
    partial_pre = partial_pre.reshape(cells_here, hidden)
    onehot = (batch_ids[:, None] == jnp.arange(BATCHES, dtype=jnp.int32)[None, :]).astype(
        jnp.float32
    )
    onehot_low = onehot.astype(jnp.bfloat16)
    enc_total = lax.psum(partial_pre, "region")
    pre_one = enc_total + matmul(onehot, trunk_rows[:BATCHES])
    (decoded, diverge), pull_back = jax.vjp(
        lambda pre_in, weights, head_part: trunk_forward(
            pre_in, weights, head_part, noise_draw, onehot
        ),
        pre_one,
        trunk_rows,
        head_rows,
    )
    decoded_low = decoded.astype(jnp.bfloat16)
    decoded_blocks = decoded_low.reshape(blocks, block_rows, hidden)
    factor_blocks = cell_factor.reshape(blocks, block_rows)
    region_bias = vec_low[0].astype(jnp.float32)
    region_logit = vec_low[1].astype(jnp.float32)
    log_region = jax.nn.log_sigmoid(region_logit)
    keep_region = jax.nn.sigmoid(-region_logit)

    def decode_block(carried, inputs):
        grad_dec, grad_bias, grad_logit, recon_sum = carried
        counts, seed_rows, hidden_low, factors = inputs
        mask_rows = region_masks(
            counts, seed_rows, first_region, regions_here, total_regions
        ).astype(jnp.float32)
        logits = jnp.dot(hidden_low, dec_low, preferred_element_type=jnp.float32) + region_bias
        log_prob = jax.nn.log_sigmoid(logits) + jnp.log(factors)[:, None] + log_region[None, :]
        probability = jnp.exp(log_prob)
        recon_sum = recon_sum - jnp.sum(
            mask_rows * log_prob + (1.0 - mask_rows) * jnp.log1p(-probability)
        )
        signal = (mask_rows - (1.0 - mask_rows) * probability / (1.0 - probability)) * loss_scale
        grad_logits = (-jax.nn.sigmoid(-logits) * signal).astype(jnp.bfloat16)
        grad_dec = grad_dec + lax.dot_general(
            hidden_low, grad_logits, (((0,), (0,)), ((), ())), preferred_element_type=jnp.float32
        )
        grad_bias = grad_bias + jnp.sum(grad_logits, axis=0, dtype=jnp.float32)
        grad_logit = grad_logit - keep_region * jnp.sum(signal, axis=0)
        back_part = lax.dot_general(
            grad_logits, dec_low, (((1,), (1,)), ((), ())), preferred_element_type=jnp.float32
        )
        return ((grad_dec, grad_bias, grad_logit, recon_sum), back_part)

    initial = (
        jnp.zeros((hidden, regions_here), jnp.float32),
        jnp.zeros((regions_here,), jnp.float32),
        jnp.zeros((regions_here,), jnp.float32),
        jnp.zeros((), jnp.float32),
    )
    (grad_dec, grad_bias, grad_logit, recon_sum), back_parts = lax.scan(
        decode_block, initial, (counts_blocks, seed_blocks, decoded_blocks, factor_blocks)
    )
    back_hidden = back_parts.reshape(cells_here, hidden)
    hidden_grad, recon_region = lax.psum((back_hidden, recon_sum), "region")
    grad_pre, grad_trunk, grad_head = pull_back((hidden_grad, jnp.float32(loss_scale)))
    pre_low = grad_pre.astype(jnp.bfloat16)
    batch_grad = lax.dot_general(
        onehot_low, pre_low, (((0,), (0,)), ((), ())), preferred_element_type=jnp.float32
    )
    grad_trunk = grad_trunk.at[:BATCHES].add(batch_grad)
    grad_trunk, grad_head, recon_all, diverge_all = lax.psum(
        (grad_trunk, grad_head, recon_region, diverge), "dp"
    )
    pre_blocks = pre_low.reshape(blocks, block_rows, hidden)

    def encode_back(carried, inputs):
        mask_rows = region_masks(
            inputs[0], inputs[1], first_region, regions_here, total_regions
        ).astype(jnp.bfloat16)
        return (
            carried
            + lax.dot_general(
                mask_rows, inputs[2], (((0,), (0,)), ((), ())), preferred_element_type=jnp.float32
            ),
            None,
        )

    grad_enc, _ = lax.scan(
        encode_back,
        jnp.zeros((regions_here, hidden), jnp.float32),
        (counts_blocks, seed_blocks, pre_blocks),
    )
    grad_vecs = jnp.stack([grad_bias, grad_logit])
    grad_enc, grad_dec, grad_vecs = (
        lax.psum_scatter(grad_enc, "dp", scatter_dimension=1, tiled=True),
        lax.psum_scatter(grad_dec, "dp", scatter_dimension=0, tiled=True),
        lax.psum_scatter(grad_vecs, "dp", scatter_dimension=0, tiled=True),
    )
    enc_first_new, enc_second_new, enc_update = lamb_moments(
        enc_weight, grad_enc, enc_first, enc_second
    )
    dec_first_new, dec_second_new, dec_update = lamb_moments(
        dec_weight, grad_dec, dec_first, dec_second
    )
    vec_first_new, vec_second_new, vec_update = lamb_moments(
        region_vecs, grad_vecs, vec_first, vec_second
    )
    update_local = weight_squares(enc_update, dec_update, vec_update, slot_rows)
    weight_sums, update_sums = lax.psum(
        (weight_squares(enc_weight, dec_weight, region_vecs, slot_rows), update_local),
        ("dp", "region"),
    )
    region_wn = jnp.sqrt(weight_sums)
    region_un = jnp.sqrt(update_sums)
    enc_new = enc_weight - learn_rate * (region_wn[0] / region_un[0]) * enc_update
    dec_new = dec_weight - learn_rate * (region_wn[1] / region_un[1]) * dec_update
    vec_ratio = jnp.where(row_index == 0, region_wn[2] / region_un[2], region_wn[3] / region_un[3])
    vecs_new = region_vecs - learn_rate * vec_ratio * vec_update
    trunk_first_new, trunk_second_new, trunk_update = lamb_moments(
        trunk_rows, grad_trunk, trunk_first, trunk_second
    )
    head_first_new, head_second_new, head_update = lamb_moments(
        head_rows, grad_head, head_first, head_second
    )
    row_edges = [
        0,
        BATCHES,
        BATCHES + hidden,
        2 * BATCHES + hidden + latent,
        2 * BATCHES + 2 * hidden + latent,
        2 * BATCHES + 2 * hidden + latent + 8,
    ]
    trunk_new, trunk_wn, trunk_un = lamb_groups(trunk_rows, trunk_update, row_edges)
    head_new, head_wn, head_un = lamb_groups(head_rows, head_update, [0, hidden + 1])
    norms = jnp.stack(
        [
            jnp.concatenate([region_wn, trunk_wn, head_wn]),
            jnp.concatenate([region_un, trunk_un, head_un]),
        ]
    )
    loss = jnp.stack([recon_all * loss_scale, diverge_all / all_cells])
    return (
        loss,
        enc_new,
        enc_first_new,
        enc_second_new,
        enc_new.astype(jnp.bfloat16),
        dec_new,
        dec_first_new,
        dec_second_new,
        dec_new.astype(jnp.bfloat16),
        vecs_new,
        vec_first_new,
        vec_second_new,
        trunk_new,
        trunk_first_new,
        trunk_second_new,
        head_new,
        head_first_new,
        head_second_new,
        norms,
    )


def solution(mesh):
    return jax.shard_map(
        on_device,
        mesh=mesh,
        in_specs=(
            P("dp"),
            P("dp"),
            P("dp"),
            P("dp", None),
            P("dp"),
            P("region", "dp"),
            P("region", "dp"),
            P("region", "dp"),
            P("dp", "region"),
            P("dp", "region"),
            P("dp", "region"),
            P("dp", "region"),
            P("dp", "region"),
            P("dp", "region"),
            P(),
            P(),
            P(),
            P(),
            P(),
            P(),
        ),
        out_specs=(
            P(),
            P("region", "dp"),
            P("region", "dp"),
            P("region", "dp"),
            P("region", "dp"),
            P("dp", "region"),
            P("dp", "region"),
            P("dp", "region"),
            P("dp", "region"),
            P("dp", "region"),
            P("dp", "region"),
            P("dp", "region"),
            P(),
            P(),
            P(),
            P(),
            P(),
            P(),
            P(),
        ),
        check_vma=False,
    )
```

profile of v0, /device:TPU:0, one launch (start us, length us, event | category | flops | bytes accessed | tf_op | source)
XLA Modules:
  0.0 877.5 jit_solution(4330750522462627467)
XLA Ops:
  13.2 2.3 broadcast.824.clone
  15.5 51.1 %while.50 = (s32[]{:T(128)}, f32[8,1024,128]{2,1,0:T(8,128)}, s32[8,1024]{1,0:T(8,128)}, s32[]{:T(128)}, s32[8,1024]{1,0:T(8,128)}, /*index=5*/bf16[768,128]{1,0:T(8,128)(2,1)S(1)}, s32[]{:T(128)}) while((s32[]{:T(128)}, f32[8,1024,128]{2,1,0:T(8,128)}, s32[8,1024]{1,0:T(8,128)}, s32[]{:T(128)}, s32[8,1024]{1,0:T(8,128)}, ...), condition=%wide.region_1.2_spmd, body=%wide.region_0.1_spmd.sunk | while | flops 215511040 | bytes 770645 | solution.py:145
  16.3 5.6 fusion.253
  22.7 5.6 fusion.253
  29.1 5.6 fusion.253
  35.5 5.6 fusion.253
  41.8 5.6 fusion.253
  48.2 5.6 fusion.253
  54.6 5.6 fusion.253
  61.0 5.6 fusion.253
  72.8 164.7 %all-reduce.26.cloned.1.call-done = f32[8192,128]{1,0:T(8,128)} async-done(((f32[8192,128]{1,0:T(8,128)}), f32[8192,128]{1,0:T(8,128)}) %all-reduce.26.cloned.1.call-update) | async-done | bytes 4194320 | tf_op jit(solution)/shard_map/psum | solution.py:153
  237.6 6.2 fusion.224
  243.8 2.4 multiply_reduce_fusion.11
  246.2 8.2 fusion.225
  254.4 5.6 copy.58
  260.0 4.3 multiply_reduce_fusion.10
  264.5 5.1 convolution_add_fusion.3
  269.6 6.7 fusion.188
  276.3 4.6 fusion.226
  281.0 2.4 multiply_reduce_fusion.9
  283.4 4.9 fusion.227
  288.3 2.4 multiply_reduce_fusion.8
  291.4 5.3 fusion.102
  299.0 146.3 %while.51 = (s32[]{:T(128)}, f32[128,768]{1,0:T(8,128)S(1)}, f32[768]{0:T(1024)S(1)}, f32[768]{0:T(1024)}, f32[]{:T(128)}, /*index=5*/f32[8,1024,128]{2,1,0:T(8,...) while((s32[]{:T(128)}, f32[128,768]{1,0:T(8,128)S(1)}, ...), condition=%wide.region_15.16_spmd.clone, body=%wide.region_11.15_spmd.clone.sunk | while | flops 643528960 | bytes 19630788 | solution.py:201
  301.0 10.9 %fusion.260 = (f32[768]{0:T(1024)}, f32[1024,768]{1,0:T(8,128)S(1)}, f32[]{:T(128)}, f32[1024,768]{1,0:T(8,128)S(1)}) fusion(f32[768]{0:T(1024)} %get-tuple-element.1021, f32[1024]{0:T(1024)S(1)} %bitcast.133, f32[768]{0:T(1024)S(1)} %get-tuple-element.1016, s32[1024]{0:T(1024)S(1)} %bitcast.134, s32[1024]{0:T(1024)S(1)} %bitcast.128, ...), kind=kOutput, calls=%fused_computation.378.clone.1 | convolution fusion | flops 234355968 | bytes 6783492 | tf_op jit(solution)/shard_map/while/body/eval_jaxpr/dot_general | solution.py:177
  319.2 10.9 %fusion.260 = (f32[768]{0:T(1024)}, f32[1024,768]{1,0:T(8,128)S(1)}, f32[]{:T(128)}, f32[1024,768]{1,0:T(8,128)S(1)}) fusion(f32[768]{0:T(1024)} %get-tuple-element.1021, f32[1024]{0:T(1024)S(1)} %bitcast.133, f32[768]{0:T(1024)S(1)} %get-tuple-element.1016, s32[1024]{0:T(1024)S(1)} %bitcast.134, s32[1024]{0:T(1024)S(1)} %bitcast.128, ...), kind=kOutput, calls=%fused_computation.378.clone.1 | convolution fusion | flops 234355968 | bytes 6783492 | tf_op jit(solution)/shard_map/while/body/eval_jaxpr/dot_general | solution.py:177
  337.5 10.9 %fusion.260 = (f32[768]{0:T(1024)}, f32[1024,768]{1,0:T(8,128)S(1)}, f32[]{:T(128)}, f32[1024,768]{1,0:T(8,128)S(1)}) fusion(f32[768]{0:T(1024)} %get-tuple-element.1021, f32[1024]{0:T(1024)S(1)} %bitcast.133, f32[768]{0:T(1024)S(1)} %get-tuple-element.1016, s32[1024]{0:T(1024)S(1)} %bitcast.134, s32[1024]{0:T(1024)S(1)} %bitcast.128, ...), kind=kOutput, calls=%fused_computation.378.clone.1 | convolution fusion | flops 234355968 | bytes 6783492 | tf_op jit(solution)/shard_map/while/body/eval_jaxpr/dot_general | solution.py:177
  355.7 10.9 %fusion.260 = (f32[768]{0:T(1024)}, f32[1024,768]{1,0:T(8,128)S(1)}, f32[]{:T(128)}, f32[1024,768]{1,0:T(8,128)S(1)}) fusion(f32[768]{0:T(1024)} %get-tuple-element.1021, f32[1024]{0:T(1024)S(1)} %bitcast.133, f32[768]{0:T(1024)S(1)} %get-tuple-element.1016, s32[1024]{0:T(1024)S(1)} %bitcast.134, s32[1024]{0:T(1024)S(1)} %bitcast.128, ...), kind=kOutput, calls=%fused_computation.378.clone.1 | convolution fusion | flops 234355968 | bytes 6783492 | tf_op jit(solution)/shard_map/while/body/eval_jaxpr/dot_general | solution.py:177
  374.0 10.9 %fusion.260 = (f32[768]{0:T(1024)}, f32[1024,768]{1,0:T(8,128)S(1)}, f32[]{:T(128)}, f32[1024,768]{1,0:T(8,128)S(1)}) fusion(f32[768]{0:T(1024)} %get-tuple-element.1021, f32[1024]{0:T(1024)S(1)} %bitcast.133, f32[768]{0:T(1024)S(1)} %get-tuple-element.1016, s32[1024]{0:T(1024)S(1)} %bitcast.134, s32[1024]{0:T(1024)S(1)} %bitcast.128, ...), kind=kOutput, calls=%fused_computation.378.clone.1 | convolution fusion | flops 234355968 | bytes 6783492 | tf_op jit(solution)/shard_map/while/body/eval_jaxpr/dot_general | solution.py:177
  392.2 10.9 %fusion.260 = (f32[768]{0:T(1024)}, f32[1024,768]{1,0:T(8,128)S(1)}, f32[]{:T(128)}, f32[1024,768]{1,0:T(8,128)S(1)}) fusion(f32[768]{0:T(1024)} %get-tuple-element.1021, f32[1024]{0:T(1024)S(1)} %bitcast.133, f32[768]{0:T(1024)S(1)} %get-tuple-element.1016, s32[1024]{0:T(1024)S(1)} %bitcast.134, s32[1024]{0:T(1024)S(1)} %bitcast.128, ...), kind=kOutput, calls=%fused_computation.378.clone.1 | convolution fusion | flops 234355968 | bytes 6783492 | tf_op jit(solution)/shard_map/while/body/eval_jaxpr/dot_general | solution.py:177
  410.4 10.9 %fusion.260 = (f32[768]{0:T(1024)}, f32[1024,768]{1,0:T(8,128)S(1)}, f32[]{:T(128)}, f32[1024,768]{1,0:T(8,128)S(1)}) fusion(f32[768]{0:T(1024)} %get-tuple-element.1021, f32[1024]{0:T(1024)S(1)} %bitcast.133, f32[768]{0:T(1024)S(1)} %get-tuple-element.1016, s32[1024]{0:T(1024)S(1)} %bitcast.134, s32[1024]{0:T(1024)S(1)} %bitcast.128, ...), kind=kOutput, calls=%fused_computation.378.clone.1 | convolution fusion | flops 234355968 | bytes 6783492 | tf_op jit(solution)/shard_map/while/body/eval_jaxpr/dot_general | solution.py:177
  428.7 10.9 %fusion.260 = (f32[768]{0:T(1024)}, f32[1024,768]{1,0:T(8,128)S(1)}, f32[]{:T(128)}, f32[1024,768]{1,0:T(8,128)S(1)}) fusion(f32[768]{0:T(1024)} %get-tuple-element.1021, f32[1024]{0:T(1024)S(1)} %bitcast.133, f32[768]{0:T(1024)S(1)} %get-tuple-element.1016, s32[1024]{0:T(1024)S(1)} %bitcast.134, s32[1024]{0:T(1024)S(1)} %bitcast.128, ...), kind=kOutput, calls=%fused_computation.378.clone.1 | convolution fusion | flops 234355968 | bytes 6783492 | tf_op jit(solution)/shard_map/while/body/eval_jaxpr/dot_general | solution.py:177
  452.9 42.5 %psum.64 = f32[]{:T(128)} all-reduce(f32[]{:T(128)} %get-tuple-element.495), channel_id=1, replica_groups=mesh['dp'=2,'region'=16] {'region'}, use_global_device_ids=true, to_apply=%region_16.17 | all-reduce | flops 1 | bytes 8 | tf_op jit(solution)/shard_map/psum | solution.py:205
  495.5 2.4 multiply_reduce_fusion.12
  497.9 130.5 %all-reduce.28.cloned.1.call-done = f32[8192,128]{1,0:T(8,128)} async-done(((f32[8192,128]{1,0:T(8,128)}), f32[8192,128]{1,0:T(8,128)}) %all-reduce.28.cloned.1.call-update) | async-done | bytes 4194320 | tf_op jit(solution)/shard_map/psum | solution.py:205
  628.4 7.6 fusion.208
  636.1 5.1 fusion.221
  641.3 6.4 multiply_reduce_fusion.2
  647.8 5.3 fusion.220
  653.2 4.5 multiply_add_fusion.9
  657.9 4.4 fusion.122
  662.3 11.4 %multiply_reduce_fusion.1 = (f32[128]{0:T(128)}, f32[8192]{0:T(1024)S(1)}, f32[128]{0:T(128)}, f32[8192,128]{1,0:T(8,128)S(1)}) fusion(f32[8192,128]{1,0:T(8,128)S(1)} %copy-done.3, f32[8192]{0:T(1024)S(1)} %copy-done.50, f32[8192]{0:T(1024)S(1)} %copy-done.29, f32[128]{0:T(128)S(1)} %copy-done.67, f32[129,20]{0,1:T(8,128)S(1)} %copy-done.44, ...), kind=kOutput, calls=%fused_computation.162 | convolution fusion | flops 267542272 | bytes 9549824 | tf_op jit(solution)/shard_map/transpose(jvp())/dot_general | solution.py:19
  673.7 11.0 %fusion.109 = f32[128,128]{1,0:T(8,128)} fusion(f32[8192,128]{1,0:T(8,128)S(1)} %get-tuple-element.698, f32[8192,128]{1,0:T(8,128)S(1)} %copy-done.7, f32[8192]{0:T(1024)S(1)} %negate_multiply_fusion.3, f32[128]{0:T(128)S(1)} %copy-done.75, f32[128]{0:T(128)S(1)} %copy-done.69, f32[8192]{0:T(1024)S(1)} %copy-done.52, f32[8192]{0:T(1024)S(1)} %copy-done.31), kind=kOutput, calls=%fused_computation.186 | convolution fusion | flops 1619001344 | bytes 8553472 | tf_op jit(solution)/shard_map/transpose(jvp())/dot_general | solution.py:19
  684.7 2.5 fusion.117
  687.2 2.7 fusion.115
  690.0 5.1 fusion.218
  695.2 8.0 multiply_reduce_fusion
  703.2 10.9 %fusion.103 = f32[128,128]{1,0:T(8,128)} fusion(f32[8192,128]{1,0:T(8,128)S(1)} %get-tuple-element.692, f32[8192,128]{1,0:T(8,128)S(1)} %copy-done.5, f32[8192]{0:T(1024)S(1)} %negate_multiply_fusion.1, f32[128]{0:T(128)S(1)} %copy-done.73, f32[128]{0:T(128)S(1)} %copy-done.65, f32[8192]{0:T(1024)S(1)} %copy-done.48, f32[8192]{0:T(1024)S(1)} %copy-done.27), kind=kOutput, calls=%fused_computation.182 | convolution fusion | flops 1619001344 | bytes 8553472 | tf_op jit(solution)/shard_map/transpose(jvp())/dot_general | solution.py:19
  714.2 8.2 fusion.217
  722.5 3.7 add_convert_fusion
  726.3 54.1 %while.52 = (s32[]{:T(128)}, f32[768,128]{1,0:T(8,128)}, s32[8,1024]{1,0:T(8,128)}, s32[]{:T(128)}, s32[8,1024]{1,0:T(8,128)}, /*index=5*/bf16[8,1024,128]{2,1,0:T(8,128)(2,1)S(1)}, s32[]{:T(128)}, s32[]{:T(128)}) while((s32[]{:T(128)}, f32[768,128]{1,0:T(8,128)}, s32[8,1024]{1,0:T(8,128)}, s32[]{:T(128)}, ...), condition=%wide.region_34.35_spmd.clone, body=%wide.region_33.34_spmd.clone.sunk | while | flops 215707648 | bytes 1099883 | solution.py:229
  727.2 5.1 fusion.265
  733.1 6.1 fusion.265
  740.0 6.1 fusion.265
  746.8 6.1 fusion.265
  753.7 6.1 fusion.265
  760.6 6.1 fusion.265
  767.5 6.1 fusion.265
  774.3 6.1 fusion.265
  783.4 4.5 all-reduce.21
  789.3 2.5 multiply_reduce_fusion.28
  807.9 3.8 reduce-scatter.3.cloned.1.call-done
  816.1 4.6 concatenate.19
  820.7 40.4 %all-reduce.20 = (f32[4]{0:T(128)S(1)}, f32[4]{0:T(128)S(1)}) all-reduce(f32[4]{0:T(128)S(1)} %pad_maximum_fusion.3, f32[4]{0:T(128)S(1)} %pad_maximum_fusion.4), channel_id=1, replica_groups=mesh['dp'=2,'region'=16] {'dp','region'}, use_global_device_ids=true, to_apply=%region_23.24 | all-reduce | flops 8 | bytes 64 | tf_op jit(solution)/shard_map/psum | solution.py:250
  (373 shorter events, 107.7 us)
Async XLA Ops:
  7.2 230.4 %all-reduce.26.cloned.1.call-start = ((), (), s32[]{:S(2)}) async-start(), calls=%async_computation.2 | async-start | bytes 8388608 | tf_op jit(solution)/shard_map/psum | solution.py:153
  66.6 5.3 copy-start.43
  66.6 5.5 copy-start.15
  66.6 171.0 %copy-start.23 = (s32[8192]{0:T(1024)S(1)}, s32[8192]{0:T(1024)}, u32[]{:S(2)}) copy-start(s32[8192]{0:T(1024)} %param.30) | copy-start | bytes 98308
  66.6 428.8 %reduce-scatter.5.cloned.1.call-start = ((), (), s32[]{:S(2)}) async-start(), calls=%async_computation.5 | async-start | bytes 589824 | tf_op jit(solution)/shard_map/reduce_scatter | solution.py:237
  72.1 174.1 %copy-start.64 = (f32[128]{0:T(128)}, f32[128]{0:T(128)S(1)}, u32[]{:S(2)}) copy-start(f32[128]{0:T(128)S(1)} %get-tuple-element.727) | copy-start | bytes 1540
  72.1 174.1 %copy-start.72 = (f32[128]{0:T(128)}, f32[128]{0:T(128)S(1)}, u32[]{:S(2)}) copy-start(f32[128]{0:T(128)S(1)} %get-tuple-element.726) | copy-start | bytes 1540
  72.2 192.3 %copy-start.66 = (f32[128]{0:T(128)}, f32[128]{0:T(128)S(1)}, u32[]{:S(2)}) copy-start(f32[128]{0:T(128)S(1)} %get-tuple-element.725) | copy-start | bytes 1540
  72.2 192.3 %copy-start.76 = (f32[128]{0:T(128)}, f32[128]{0:T(128)S(1)}, u32[]{:S(2)}) copy-start(f32[128]{0:T(128)S(1)} %get-tuple-element.724) | copy-start | bytes 1540
  72.2 211.2 %copy-start.68 = (f32[128]{0:T(128)}, f32[128]{0:T(128)S(1)}, u32[]{:S(2)}) copy-start(f32[128]{0:T(128)S(1)} %get-tuple-element.723) | copy-start | bytes 1540
  72.2 211.2 %copy-start.74 = (f32[128]{0:T(128)}, f32[128]{0:T(128)S(1)}, u32[]{:S(2)}) copy-start(f32[128]{0:T(128)S(1)} %get-tuple-element.722) | copy-start | bytes 1540
  72.2 218.6 %copy-start.60 = (f32[128]{0:T(128)}, f32[128]{0:T(128)S(1)}, u32[]{:S(2)}) copy-start(f32[128]{0:T(128)S(1)} %get-tuple-element.720) | copy-start | bytes 1540
  72.2 218.6 %copy-start.62 = (f32[128]{0:T(128)}, f32[128]{0:T(128)S(1)}, u32[]{:S(2)}) copy-start(f32[128]{0:T(128)S(1)} %get-tuple-element.721) | copy-start | bytes 1540
  243.7 10.7 %copy-start.4 = (f32[8192,128]{1,0:T(8,128)}, f32[8192,128]{1,0:T(8,128)S(1)}, u32[]{:S(2)}) copy-start(f32[8192,128]{1,0:T(8,128)S(1)} %get-tuple-element.738) | copy-start | bytes 12582916
  243.8 10.7 %copy-start.26 = (f32[8192]{0:T(1024)}, f32[8192]{0:T(1024)S(1)}, u32[]{:S(2)}) copy-start(f32[8192]{0:T(1024)S(1)} %broadcast_multiply_fusion.3) | copy-start | bytes 98308
  246.2 8.3 copy-start.32
  246.2 8.2 copy-start.47
  260.0 9.5 %copy-start.28 = (f32[8192]{0:T(1024)}, f32[8192]{0:T(1024)S(1)}, u32[]{:S(2)}) copy-start(f32[8192]{0:T(1024)S(1)} %broadcast_multiply_fusion.2) | copy-start | bytes 98308
  280.9 7.3 copy-start.6
  280.9 7.3 copy-start.30
  288.3 8.4 copy-start
  290.7 8.3 copy-start.38
  445.3 6.9 copy-start.82
  445.3 50.1 %copy-start.46 = (f32[768]{0:T(1024)S(1)}, f32[768]{0:T(1024)}, u32[]{:S(2)}) copy-start(f32[768]{0:T(1024)} %get-tuple-element.500) | copy-start | bytes 9220
  445.3 50.1 %copy-start.12 = (f32[64,768]{1,0:T(8,128)S(1)}, f32[64,768]{1,0:T(8,128)}, u32[]{:S(2)}) copy-start(f32[64,768]{1,0:T(8,128)} %param.36) | copy-start | bytes 589828
  445.3 50.1 %copy-start.40 = (f32[64,768]{1,0:T(8,128)S(1)}, f32[64,768]{1,0:T(8,128)}, u32[]{:S(2)}) copy-start(f32[64,768]{1,0:T(8,128)} %param.38) | copy-start | bytes 589828
  445.4 50.1 %copy-start.41 = (f32[64,768]{1,0:T(8,128)S(1)}, f32[64,768]{1,0:T(8,128)}, u32[]{:S(2)}) copy-start(f32[64,768]{1,0:T(8,128)} %param.37) | copy-start | bytes 589828
  445.4 183.0 %copy-start.25 = (f32[8192]{0:T(1024)S(1)}, f32[8192]{0:T(1024)}, u32[]{:S(2)}) copy-start(f32[8192]{0:T(1024)} %copy-done.24) | copy-start | bytes 98308
  445.4 183.0 %copy-start.61 = (f32[128]{0:T(128)S(1)}, f32[128]{0:T(128)}, u32[]{:S(2)}) copy-start(f32[128]{0:T(128)} %copy-done.60) | copy-start | bytes 1540
  445.4 183.0 %copy-start.63 = (f32[128]{0:T(128)S(1)}, f32[128]{0:T(128)}, u32[]{:S(2)}) copy-start(f32[128]{0:T(128)} %copy-done.62) | copy-start | bytes 1540
  446.1 182.3 %all-reduce.28.cloned.1.call-start = ((), (), s32[]{:S(2)}) async-start(), calls=%async_computation.3 | async-start | bytes 8388608 | tf_op jit(solution)/shard_map/psum | solution.py:205
  446.8 353.6 %all-reduce.30.cloned.1.call-start = ((), (), s32[]{:S(2)}) async-start(), calls=%async_computation.6 | async-start | bytes 303104 | tf_op jit(solution)/shard_map/psum | solution.py:212
  497.9 138.1 %copy-start.39 = (f32[8192]{0:T(1024)S(1)}, f32[8192]{0:T(1024)}, u32[]{:S(2)}) copy-start(f32[8192]{0:T(1024)} %copy-done.38) | copy-start | bytes 98308
  628.4 7.6 copy-start.1
  628.4 7.6 copy-start.8
  636.1 5.2 copy-start.7
  636.1 5.2 copy-start.31
  636.1 5.2 copy-start.52
  636.1 5.2 copy-start.69
  636.1 5.2 copy-start.75
  641.3 6.4 copy-start.37
  684.7 5.2 copy-start.35
  703.2 11.0 %copy-start.33 = (f32[8192]{0:T(1024)S(1)}, f32[8192]{0:T(1024)}, u32[]{:S(2)}) copy-start(f32[8192]{0:T(1024)} %copy-done.32) | copy-start | bytes 98308
  726.2 54.2 %copy-start.59 = (f32[8,128]{1,0:T(8,128)S(1)}, f32[8,128]{1,0:T(8,128)}, u32[]{:S(2)}) copy-start(f32[8,128]{1,0:T(8,128)} %fusion.117) | copy-start | bytes 12292
  726.2 54.3 %copy-start.70 = (f32[128]{0:T(128)S(1)}, f32[128]{0:T(128)}, u32[]{:S(2)}) copy-start(f32[128]{0:T(128)} %get-tuple-element.582) | copy-start | bytes 1540
  726.2 54.3 %copy-start.71 = (f32[128]{0:T(128)S(1)}, f32[128]{0:T(128)}, u32[]{:S(2)}) copy-start(f32[128]{0:T(128)} %get-tuple-element.583) | copy-start | bytes 1540
  726.2 54.3 %copy-start.78 = (f32[128]{0:T(128)S(1)}, f32[128]{0:T(128)}, u32[]{:S(2)}) copy-start(f32[128]{0:T(128)} %get-tuple-element.585) | copy-start | bytes 1540
  726.3 54.2 %copy-start.79 = (f32[128]{0:T(128)S(1)}, f32[128]{0:T(128)}, u32[]{:S(2)}) copy-start(f32[128]{0:T(128)} %get-tuple-element.591) | copy-start | bytes 1540
  726.3 54.2 %copy-start.80 = (f32[128]{0:T(128)S(1)}, f32[128]{0:T(128)}, u32[]{:S(2)}) copy-start(f32[128]{0:T(128)} %get-tuple-element.587) | copy-start | bytes 1540
  726.3 54.2 %copy-start.81 = (f32[128]{0:T(128)S(1)}, f32[128]{0:T(128)}, u32[]{:S(2)}) copy-start(f32[128]{0:T(128)} %get-tuple-element.592) | copy-start | bytes 1540
  726.3 54.3 %copy-start.55 = (f32[128,128]{1,0:T(8,128)S(1)}, f32[128,128]{1,0:T(8,128)}, u32[]{:S(2)}) copy-start(f32[128,128]{1,0:T(8,128)} %fusion.109) | copy-start | bytes 196612
  726.3 61.6 %copy-start.45 = (f32[129,20]{0,1:T(8,128)S(1)}, f32[129,20]{0,1:T(8,128)}, u32[]{:S(2)}) copy-start(f32[129,20]{0,1:T(8,128)} %param.45) | copy-start | bytes 30964
  726.3 63.0 %copy-start.58 = (f32[1,768]{1,0:T(1,128)S(1)}, f32[1,768]{1,0:T(1,128)}, u32[]{:S(2)}) copy-start(f32[1,768]{1,0:T(1,128)} %param.39) | copy-start | bytes 9220
  780.4 20.1 %copy-start.17 = (f32[290,128]{1,0:T(8,128)S(1)}, f32[290,128]{1,0:T(8,128)}, u32[]{:S(2)}) copy-start(f32[290,128]{1,0:T(8,128)} %param.42) | copy-start | bytes 445444
  780.4 31.3 %copy-start.14 = (f32[768,64]{0,1:T(8,128)S(1)}, f32[768,64]{0,1:T(8,128)}, u32[]{:S(2)}) copy-start(f32[768,64]{0,1:T(8,128)} %param.33) | copy-start | bytes 589828
  780.4 31.3 %copy-start.42 = (f32[768,64]{0,1:T(8,128)S(1)}, f32[768,64]{0,1:T(8,128)}, u32[]{:S(2)}) copy-start(f32[768,64]{0,1:T(8,128)} %param.35) | copy-start | bytes 589828
  780.4 88.5 %copy-start.13 = (f32[64,768]{1,0:T(8,128)S(1)}, f32[64,768]{1,0:T(8,128)}, u32[]{:S(2)}) copy-start(f32[64,768]{1,0:T(8,128)} %param.36) | copy-start | bytes 589828
  780.4 88.5 %copy-start.18 = (f32[64,768]{1,0:T(8,128)S(1)}, f32[64,768]{1,0:T(8,128)}, u32[]{:S(2)}) copy-start(f32[64,768]{1,0:T(8,128)} %get-tuple-element.693) | copy-start | bytes 589828
  780.4 88.5 %copy-start.19 = (f32[64,768]{1,0:T(8,128)S(1)}, f32[64,768]{1,0:T(8,128)}, u32[]{:S(2)}) copy-start(f32[64,768]{1,0:T(8,128)} %get-tuple-element.694) | copy-start | bytes 589828
  783.4 28.3 %reduce-scatter.3.cloned.1.call-start = ((), (), s32[]{:S(2)}) async-start(), calls=%async_computation.4 | async-start | bytes 589824 | tf_op jit(solution)/shard_map/reduce_scatter | solution.py:236
  789.3 81.2 %copy-start.53 = (f32[129,20]{0,1:T(8,128)}, f32[129,20]{0,1:T(8,128)S(1)}, u32[]{:S(2)}) copy-start(f32[129,20]{0,1:T(8,128)S(1)} %get-tuple-element.674) | copy-start | bytes 30964
  789.3 81.2 %copy-start.54 = (f32[129,20]{0,1:T(8,128)}, f32[129,20]{0,1:T(8,128)S(1)}, u32[]{:S(2)}) copy-start(f32[129,20]{0,1:T(8,128)S(1)} %get-tuple-element.675) | copy-start | bytes 30964
  813.5 57.1 %copy-start.20 = (f32[768,64]{0,1:T(8,128)}, f32[768,64]{0,1:T(8,128)S(1)}, u32[]{:S(2)}) copy-start(f32[768,64]{0,1:T(8,128)S(1)} %get-tuple-element.687) | copy-start | bytes 589828
  813.5 57.1 %copy-start.21 = (f32[768,64]{0,1:T(8,128)}, f32[768,64]{0,1:T(8,128)S(1)}, u32[]{:S(2)}) copy-start(f32[768,64]{0,1:T(8,128)S(1)} %get-tuple-element.688) | copy-start | bytes 589828
  (24 other events, 91.7 us)
Sparse Core Ops, SparseCore 0:
  66.8 170.7 all-reduce.25
  446.2 6.7 reduce-scatter.4
  458.6 169.7 all-reduce.27
  783.5 16.9 all-reduce.29
  802.6 8.9 reduce-scatter.2
where the time goes:
time: 888 us; the launch traced here: 878 us
  waiting for transfers between devices  301 us (34%)
  matrix products  299 us (34%)
  other arithmetic  95.9 us (11%)
  blocking collectives  93.3 us (11%)
  local copies, waits for them, and re-layouts  50 us (6%)
  between operations  31.4 us (4%)
    psum x1, waiting for transfers between devices, on_device(): enc_total = lax.psum(partial_pre, 'region')  165 us
    psum x1, waiting for transfers between devices, on_device(): hidden_grad, recon_region = lax.psum((back_hidden, recon_sum), 'region')  131 us
    dot_general x15, matrix products, matmul(): jnp.dot(left, right, precision=highest, preferred_element_type=jnp.float32)  97.4 us
    dot_general x8, matrix products, decode_block(): jnp.dot(hidden_low, dec_low, preferred_element_type=jnp.float32)  87 us
    dot_general x8, matrix products, encode_back(): lax.dot_general(mask_rows, inputs[2], (((0,), (0,)), ((), ())), preferred...  47.4 us
    dot_general x8, matrix products, encode_block(): jnp.dot(mask_rows, enc_low, preferred_element_type=jnp.float32)  44.5 us
    psum x1, blocking collectives, on_device(): hidden_grad, recon_region = lax.psum((back_hidden, recon_sum), 'region')  42.5 us
    psum x1, blocking collectives, on_device(): lax.psum((weight_squares(enc_weight, dec_weight, region_vecs, slot_rows),...  40.4 us
  transfers between devices with their start and end apart: 5, of which 4 were waited for; matrix products, arithmetic and copies ran while one was open for 2% of the time, Pallas kernels for 0%

commit v1 on v0

v1 whole, which is shorter than its diff:
```python
import functools

import jax
import jax.numpy as jnp
from jax import lax
from jax.experimental import pallas as pl
from jax.experimental.pallas import tpu as pltpu
from jax.sharding import Mesh
from jax.sharding import PartitionSpec as P

BATCHES = 8
COLUMNS = 4

norm_eps = 1e-05
leak_slope = 0.01
decay_rate = 0.5
weight_decay = 0.01
learn_rate = 0.5
lamb_eps = 1e-12

f32 = jnp.float32
bf16 = jnp.bfloat16
VMEM = pl.BlockSpec(memory_space=pltpu.VMEM)
SMEM = pl.BlockSpec(memory_space=pltpu.SMEM)
MEGA = 1024 * 1024


def params(mib=48):
    return pltpu.CompilerParams(vmem_limit_bytes=mib * MEGA)


def cost(flops, moved, transcendentals=0):
    return pl.CostEstimate(flops=flops, bytes_accessed=moved, transcendentals=transcendentals)


def exact(left, right, contract=((1,), (0,))):
    return lax.dot_general(
        left, right, (contract, ((), ())), precision=lax.Precision.HIGHEST, preferred_element_type=f32
    )


def wide(left, right, contract=((1,), (0,))):
    return lax.dot_general(left, right, (contract, ((), ())), preferred_element_type=f32)


def remainder(values, divisor):
    guess = jnp.floor(values.astype(f32) * (1.0 / divisor)).astype(jnp.int32)
    rest = values - guess * divisor
    rest = jnp.where(rest < 0, rest + divisor, rest)
    return jnp.where(rest >= divisor, rest - divisor, rest)


def turns(values, total):
    whole = 2**32 // total
    part = (2**32 % total) / total
    return values * whole + (values.astype(f32) * part + 0.5).astype(jnp.int32)


def mask_kernel(total, width, base_ref, cells_ref, mask_ref, factor_ref):
    step = pl.program_id(0)
    counts = cells_ref[0, pl.ds(step, 1), :].astype(jnp.int32)
    seeds = cells_ref[1, pl.ds(step, 1), :].astype(jnp.int32)
    factors = cells_ref[2, pl.ds(step, 1), :]
    stride = 6 * remainder(seeds, total // 6) + 1
    rows = []
    for column in range(COLUMNS):
        base = base_ref[column]
        upper = remainder(stride * (base // 256), total)
        rows.append(remainder(upper * 256 + stride * (base % 256) + seeds, total))
    low_end = jnp.int32(-(2**31))
    rows.append(stride)
    rows.append(turns(remainder(stride * 128, total), total))
    rows.append(turns(counts, total) + low_end)
    rows.append(counts)
    table = jnp.concatenate(rows, axis=0).T
    factor_ref[...] = jnp.broadcast_to(
        jnp.broadcast_to(factors, (8, 128)).T[:, 0:1], (128, 128)
    )
    half = 2**31 // total
    for part in range(2):
        lines = slice(part * 64, part * 64 + 64)
        shape = (64, 128)
        lane = lax.broadcasted_iota(jnp.int32, shape, 1)
        span = jnp.broadcast_to(table[lines, 4:5], shape) * lane
        advance = jnp.broadcast_to(table[lines, 5:6], shape)
        limit = jnp.broadcast_to(table[lines, 6:7], shape)
        for column in range(COLUMNS):
            start = remainder(jnp.broadcast_to(table[lines, column : column + 1], shape) + span, total)
            place = turns(start, total) + (low_end + jnp.int32(half))
            for group in range(width // 128):
                at = column * width + group * 128
                mask_ref[lines, at : at + 128] = jnp.where(place < limit, 1.0, 0.0).astype(bf16)
                place = place + advance


def encode_kernel(width, mask_ref, *refs):
    out_ref = refs[-1]
    total = None
    for column in range(COLUMNS):
        block = jnp.concatenate([refs[2 * column][...], refs[2 * column + 1][...]], axis=0)
        term = wide(mask_ref[:, column * width : (column + 1) * width], block, ((1,), (1,)))
        total = term if total is None else total + term
    out_ref[...] = total


def pack_kernel(info_ref, *refs):
    weight_ref, line_ref = refs[-2:]
    is_first = info_ref[0] == 0
    for column in range(COLUMNS):
        mine = refs[2 * column][...]
        other = refs[2 * column + 1][...]
        mine_line = mine[64:80].astype(f32)[0:1]
        other_line = other[64:80].astype(f32)[0:1]
        bias = jnp.where(is_first, mine_line, other_line)
        logit = jnp.where(is_first, other_line, mine_line)
        width = mine.shape[1]
        row = lax.broadcasted_iota(jnp.int32, (16, width), 0)
        weight_ref[column, 0:64] = mine[0:64]
        weight_ref[column, 64:128] = other[0:64]
        weight_ref[column, 128:144] = jnp.where(row == 0, bias, 0.0).astype(bf16)
        weight_ref[column, 144:256] = jnp.zeros((112, width), bf16)
        spread = jnp.exp(-jnp.abs(logit))
        chance = jnp.where(logit >= 0, 1.0, spread) / (1.0 + spread)
        logs = jnp.minimum(logit, 0.0) - jnp.log(1.0 + spread)
        line_ref[column, 0:16] = jnp.broadcast_to(chance, (16, width))
        line_ref[column, 16:32] = jnp.broadcast_to(logs, (16, width))


def normalize(values):
    centre = values - jnp.mean(values, axis=-1, keepdims=True)
    spread = jnp.mean(centre * centre, axis=-1, keepdims=True)
    scale = lax.rsqrt(spread + norm_eps)
    return centre * scale, scale


def leaky(values):
    return jnp.where(values >= 0, values, leak_slope * values)


def swap_halves(values, is_first):
    return jnp.where(is_first, values, pltpu.roll(values, 64, 1))


class Rows:
    def __init__(self, hidden, latent):
        self.enc_two = BATCHES
        self.dec_one = BATCHES + hidden
        self.dec_two = 2 * BATCHES + hidden + latent
        self.gain = 2 * BATCHES + 2 * hidden + latent
        self.shift = self.gain + 4
        self.end = self.gain + 8


def forward_kernel(parts, latent, own, *refs):
    info_ref, ids_ref, noise_ref, trunk_ref, head_ref, cells_ref = refs[:6]
    part_refs = refs[6 : 6 + parts]
    low_ref, norm_ref, scale_ref, left_ref, moment_ref, stat_ref = refs[6 + parts :]
    is_first = info_ref[0] == 0
    rows = Rows(128, latent)
    total = part_refs[0][...]
    for ref in part_refs[1:]:
        total = total + ref[...]
    total = swap_halves(total, is_first)
    lane = lax.broadcasted_iota(jnp.int32, total.shape, 1)
    ids = ids_ref[...]
    hot = jnp.where(lane == ids, 1.0, 0.0)
    gains = trunk_ref[rows.gain : rows.gain + 4, :]
    shifts = trunk_ref[rows.shift : rows.shift + 4, :]

    def act(index, values):
        normal, scale = normalize(values)
        norm_ref[index] = normal
        return leaky(normal * gains[index : index + 1] + shifts[index : index + 1]), scale

    first, scale0 = act(0, total + exact(hot, trunk_ref[0:128, :]))
    second, scale1 = act(1, exact(first, trunk_ref[rows.enc_two : rows.enc_two + 128, :]))
    moments = exact(second, head_ref[0:128, :]) + head_ref[128:129, :]
    inside = lane < latent
    centre = jnp.where(inside, moments, 0.0)
    log_var = jnp.where(inside, pltpu.roll(moments, 128 - latent, 1), 0.0)
    sample = centre + jnp.exp(0.5 * log_var) * noise_ref[...]
    left = sample + jnp.where(lane == ids + latent, 1.0, 0.0)
    third, scale2 = act(2, exact(left, trunk_ref[rows.dec_one : rows.dec_one + 128, :]))
    fourth, scale3 = act(3, exact(third, trunk_ref[rows.dec_two : rows.dec_two + 128, :]))
    low_ref[...] = swap_halves(fourth, is_first).astype(bf16)
    left_ref[...] = left
    moment_ref[0] = centre
    moment_ref[1] = log_var
    scale_ref[...] = jnp.where(
        lane == 0, scale0, jnp.where(lane == 1, scale1, jnp.where(lane == 2, scale2, scale3))
    )
    diverge = 0.5 * jnp.sum(jnp.exp(log_var) + centre * centre - 1.0 - log_var)
    lines = cells_ref.shape[1]
    place = lax.broadcasted_iota(jnp.int32, (lines, 128), 0) * 128 + lax.broadcasted_iota(
        jnp.int32, (lines, 128), 1
    )
    known = jnp.sum(jnp.where(place < own, cells_ref[0] * jnp.log(cells_ref[2]), 0.0))
    stat_lane = lax.broadcasted_iota(jnp.int32, (8, 128), 1)
    stat_row = lax.broadcasted_iota(jnp.int32, (8, 128), 0)
    stats = jnp.where(stat_lane == 8, known, jnp.where(stat_lane == 9, diverge, 0.0))
    stat_ref[...] = jnp.where(stat_row == 0, stats, 0.0)


def decode_kernel(loss_scale, has_sum, *refs):
    info_ref, low_ref, mask_ref, factor_ref, weight_ref, line_ref = refs[:6]
    refs = refs[6:]
    if has_sum:
        mine_in, other_in = refs[:2]
        refs = refs[2:]
    mine_ref, other_ref, back_ref, loss_ref, logit_ref, grad_ref, left_ref, turned_ref = refs
    column = pl.program_id(0)
    cells, width = grad_ref.shape
    is_first = info_ref[0] == 0

    @pl.when(column == 0)
    def _():
        low = low_ref[...]
        left_ref[:, 0:128] = low
        lane = lax.broadcasted_iota(jnp.int32, (cells, 128), 1)
        left_ref[:, 128:256] = jnp.where(lane == 0, 1.0, 0.0).astype(bf16)
        turned_ref[0:128, :] = low.astype(f32).T.astype(bf16)
        row = lax.broadcasted_iota(jnp.int32, (16, cells), 0)
        turned_ref[128:144, :] = jnp.where(row == 0, 1.0, 0.0).astype(bf16)

    logit_ref[...] = wide(left_ref[...], weight_ref[0])

    def step(index, carried):
        loss_sum, *signals = carried
        at = pl.ds(pl.multiple_of(index * 16, 16), 16)
        factor = factor_ref[at, :]
        top = bottom = held = None
        result = []
        for group in range(width // 128):
            lanes = slice(group * 128, group * 128 + 128)
            logits = logit_ref[at, lanes]
            spread = jnp.exp(-jnp.abs(logits))
            whole = 1.0 + spread
            positive = logits >= 0
            chance = factor * line_ref[0, 0:16, lanes]
            taken = chance * jnp.where(positive, 1.0, spread)
            opened = mask_ref[at, lanes].astype(f32) > 0.5
            rest = jnp.where(opened, 1.0, whole - taken)
            inverse = pl.reciprocal(whole * rest, approx=False)
            small = spread * loss_scale
            numerator = jnp.where(opened, jnp.where(positive, -small, -loss_scale), small * chance)
            grad_ref[at, lanes] = (numerator * inverse).astype(bf16)
            signal = jnp.where(opened, -1.0, taken * whole * inverse)
            result.append(signals[group] - (signal[0:8] + signal[8:16]))
            likely = jnp.where(opened, jnp.minimum(logits, 0.0) + line_ref[0, 16:32, lanes], 0.0)
            held = likely if held is None else held + likely
            top = rest if top is None else top * rest
            bottom = whole if bottom is None else bottom * whole
        held = held + (jnp.log(top) - jnp.log(bottom))
        return (loss_sum + (held[0:8] + held[8:16]), *result)

    zero = jnp.zeros((8, 128), f32)
    loss_sum, *signals = lax.fori_loop(0, cells // 16, step, (zero,) * (1 + width // 128))
    signal_line = jnp.sum(jnp.concatenate(signals, axis=1), axis=0, keepdims=True)
    product = wide(turned_ref[...], grad_ref[...])
    bias_line = product[128:129]
    mine_line = jnp.where(is_first, bias_line, signal_line)
    other_line = jnp.where(is_first, signal_line, bias_line)
    row = lax.broadcasted_iota(jnp.int32, (8, width), 0)
    mine_tail = jnp.where(row == 0, mine_line, 0.0)
    other_tail = jnp.where(row == 0, other_line, 0.0)
    if has_sum:
        mine_ref[0, 0:64] = mine_in[0, 0:64] + product[0:64]
        other_ref[0, 0:64] = other_in[0, 0:64] + product[64:128]
        mine_ref[0, 64:72] = mine_in[0, 64:72] + mine_tail
        other_ref[0, 64:72] = other_in[0, 64:72] + other_tail
    else:
        mine_ref[0, 0:64] = product[0:64]
        other_ref[0, 0:64] = product[64:128]
        mine_ref[0, 64:72] = mine_tail
        other_ref[0, 64:72] = other_tail
    back = wide(grad_ref[...], weight_ref[0, 0:128], ((1,), (1,)))

    @pl.when(column == 0)
    def _():
        back_ref[...] = back
        loss_ref[...] = loss_sum

    @pl.when(column > 0)
    def _():
        back_ref[...] += back
        loss_ref[...] += loss_sum


def backward_kernel(parts, latent, loss_scale, *refs):
    info_ref, ids_ref, noise_ref, trunk_ref, head_ref = refs[:5]
    norm_ref, scale_ref, left_ref, moment_ref = refs[5:9]
    part_refs = refs[9 : 9 + parts]
    low_ref, mine_ref, other_ref, sum_ref = refs[9 + parts :]
    is_first = info_ref[0] == 0
    rows = Rows(128, latent)
    total = part_refs[0][...]
    for ref in part_refs[1:]:
        total = total + ref[...]
    total = swap_halves(total, is_first)
    lane = lax.broadcasted_iota(jnp.int32, total.shape, 1)
    ids = ids_ref[...]
    gains = trunk_ref[rows.gain : rows.gain + 4, :]
    shifts = trunk_ref[rows.shift : rows.shift + 4, :]
    sum_ref[...] = jnp.zeros_like(sum_ref)
    rows_in, rows_out = ((0,), (0,)), ((1,), (1,))

    def output(index):
        return leaky(norm_ref[index] * gains[index : index + 1] + shifts[index : index + 1])

    def pull(index, grad):
        normal = norm_ref[index]
        gain = gains[index : index + 1]
        before = normal * gain + shifts[index : index + 1]
        grad = jnp.where(before >= 0, grad, leak_slope * grad)
        at = rows.gain + index
        sum_ref[at : at + 1, :] = jnp.sum(grad * normal, axis=0, keepdims=True)
        at = rows.shift + index
        sum_ref[at : at + 1, :] = jnp.sum(grad, axis=0, keepdims=True)
        grad = grad * gain
        plain = jnp.mean(grad, axis=-1, keepdims=True)
        along = jnp.mean(grad * normal, axis=-1, keepdims=True)
        return (grad - plain - normal * along) * scale_ref[:, index : index + 1]

    grad = pull(3, total)
    sum_ref[rows.dec_two : rows.dec_two + 128, :] = exact(output(2), grad, rows_in)
    grad = pull(2, exact(grad, trunk_ref[rows.dec_two : rows.dec_two + 128, :], rows_out))
    one = exact(left_ref[...], grad, rows_in)
    sum_ref[rows.dec_one : rows.dec_two, :] = one[0 : rows.dec_two - rows.dec_one]
    grad = exact(grad, trunk_ref[rows.dec_one : rows.dec_one + 128, :], rows_out)
    inside = lane < latent
    grad = jnp.where(inside, grad, 0.0)
    centre, log_var = moment_ref[0], moment_ref[1]
    grad_centre = grad + loss_scale * centre
    grad_log = grad * 0.5 * jnp.exp(0.5 * log_var) * noise_ref[...] + (0.5 * loss_scale) * (
        jnp.exp(log_var) - 1.0
    )
    both = jnp.where(inside, grad_centre, pltpu.roll(jnp.where(inside, grad_log, 0.0), latent, 1))
    head = exact(both, output(1), rows_in)
    sum_ref[296 : 296 + 24, :] = head[0:24]
    sum_ref[296 + 2 * latent : 297 + 2 * latent, :] = jnp.sum(both, axis=0, keepdims=True)
    grad = pull(1, exact(both, head_ref[0:128, :], rows_out))
    sum_ref[rows.enc_two : rows.enc_two + 128, :] = exact(output(0), grad, rows_in)
    grad = pull(0, exact(grad, trunk_ref[rows.enc_two : rows.enc_two + 128, :], rows_out))
    low = grad.astype(bf16)
    hot = jnp.where(lane == ids, 1.0, 0.0).astype(bf16)
    sum_ref[0:BATCHES, :] = wide(hot, low, rows_in)[0:BATCHES]
    low_ref[...] = swap_halves(low.astype(f32), is_first).astype(bf16)
    middle = sum_ref.shape[0] // 2
    upper, lower = sum_ref[0:middle, :], sum_ref[middle:, :]
    mine_ref[...] = jnp.where(is_first, upper, lower)
    other_ref[...] = jnp.where(is_first, lower, upper)


def encode_back_kernel(groups, mask_ref, *refs):
    low_refs = refs[:groups]
    mine_ref, other_ref, turned_ref = refs[groups:]
    cells = low_refs[0].shape[0]

    @pl.when(pl.program_id(0) == 0)
    def _():
        for group in range(groups):
            turned_ref[:, group * cells : (group + 1) * cells] = (
                low_refs[group][...].astype(f32).T.astype(bf16)
            )

    product = wide(turned_ref[...], mask_ref[...])
    mine_ref[0] = product[0:64]
    other_ref[0] = product[64:128]


def stat_tile(pairs):
    lane = lax.broadcasted_iota(jnp.int32, (8, 128), 1)
    row = lax.broadcasted_iota(jnp.int32, (8, 128), 0)
    tile = jnp.zeros((8, 128), f32)
    for index, value in pairs:
        tile = jnp.where(lane == index, value, tile)
    return jnp.where(row == 0, tile, 0.0)


def moments_of(weight, grad, first, second):
    first_new = decay_rate * first + (1.0 - decay_rate) * grad
    second_new = decay_rate * second + (1.0 - decay_rate) * grad * grad
    update = first_new / (jnp.sqrt(second_new) + lamb_eps) + weight_decay * weight
    return first_new, second_new, update


def enc_lamb_kernel(parts, *refs):
    weight_ref, first_ref, second_ref = refs[:3]
    part_refs = refs[3 : 3 + parts]
    first_out, second_out, update_out, stat_out = refs[3 + parts :]
    grad = part_refs[0][...]
    for ref in part_refs[1:]:
        grad = grad + ref[...]
    weight = weight_ref[...]
    first, second, update = moments_of(weight, grad.T, first_ref[...], second_ref[...])
    first_out[...] = first
    second_out[...] = second
    update_out[...] = update
    stat_out[...] = stat_tile([(0, jnp.sum(weight * weight)), (4, jnp.sum(update * update))])


def dec_lamb_kernel(parts, loss_scale, *refs):
    info_ref, weight_ref, first_ref, second_ref, vec_ref, vec_first_ref, vec_second_ref = refs[:7]
    part_refs = refs[7 : 7 + parts]
    first_out, second_out, update_out, vec_first_out, vec_second_out, vec_update_out, stat_out = refs[
        7 + parts :
    ]
    grad = part_refs[0][...]
    for ref in part_refs[1:]:
        grad = grad + ref[...]
    weight = weight_ref[...]
    first, second, update = moments_of(weight, grad[0:64], first_ref[...], second_ref[...])
    first_out[...] = first
    second_out[...] = second
    update_out[...] = update
    is_first = info_ref[0] == 0
    vec = vec_ref[...]
    low = vec.astype(bf16).astype(f32)
    line = grad[64:65]
    keep = 1.0 / (1.0 + jnp.exp(low))
    line = jnp.where(is_first, line, -keep * (line * loss_scale))
    vec_one, vec_two, vec_update = moments_of(vec, line, vec_first_ref[...], vec_second_ref[...])
    vec_first_out[...] = vec_one
    vec_second_out[...] = vec_two
    vec_update_out[...] = vec_update
    vec_square = jnp.sum(vec * vec)
    update_square = jnp.sum(vec_update * vec_update)
    stat_out[...] = stat_tile(
        [
            (1, jnp.sum(weight * weight)),
            (2, jnp.where(is_first, vec_square, 0.0)),
            (3, jnp.where(is_first, 0.0, vec_square)),
            (5, jnp.sum(update * update)),
            (6, jnp.where(is_first, update_square, 0.0)),
            (7, jnp.where(is_first, 0.0, update_square)),
        ]
    )


def trunk_lamb_kernel(latent, *refs):
    info_ref, mine_ref, other_ref = refs[:3]
    weight_ref, first_ref, second_ref, head_ref, head_first_ref, head_second_ref = refs[3:9]
    new_out, first_out, second_out, head_out, head_first_out, head_second_out, stat_out = refs[9:16]
    sum_ref = refs[16]
    is_first = info_ref[0] == 0
    rows = Rows(128, latent)
    mine, other = mine_ref[...], other_ref[...]
    middle = mine.shape[0]
    sum_ref[0:middle] = jnp.where(is_first, mine, other)
    sum_ref[middle : 2 * middle] = jnp.where(is_first, other, mine)
    weight = weight_ref[...]
    count = weight.shape[0]
    first, second, update = moments_of(weight, sum_ref[0:count], first_ref[...], second_ref[...])
    first_out[...] = first
    second_out[...] = second
    edges = [0, rows.enc_two, rows.dec_one, rows.dec_two, rows.gain, rows.end]
    row = lax.broadcasted_iota(jnp.int32, (count, 1), 0)
    weight_lines = jnp.sum(weight * weight, axis=1, keepdims=True)
    update_lines = jnp.sum(update * update, axis=1, keepdims=True)
    ratio = jnp.zeros((count, 1), f32)
    pairs = []
    for index in range(5):
        chosen = (row >= edges[index]) & (row < edges[index + 1])
        weight_norm = jnp.sqrt(jnp.sum(jnp.where(chosen, weight_lines, 0.0), keepdims=True))
        update_norm = jnp.sqrt(jnp.sum(jnp.where(chosen, update_lines, 0.0), keepdims=True))
        ratio = jnp.where(chosen, learn_rate * (weight_norm / update_norm), ratio)
        pairs += [(index, weight_norm), (8 + index, update_norm)]
    new_out[...] = weight - ratio * update
    size = 2 * latent
    head = head_ref[...]
    block = sum_ref[296:320]
    turned = jnp.concatenate([block, jnp.zeros((104, 128), f32)], axis=0).T[:, 0:size]
    grad_head = jnp.concatenate([turned, block[size : size + 1, 0:size]], axis=0)
    first, second, update = moments_of(head, grad_head, head_first_ref[...], head_second_ref[...])
    head_first_out[...] = first
    head_second_out[...] = second
    weight_norm = jnp.sqrt(jnp.sum(head * head, keepdims=True))
    update_norm = jnp.sqrt(jnp.sum(update * update, keepdims=True))
    head_out[...] = head - learn_rate * (weight_norm / update_norm) * update
    pairs += [(5, weight_norm), (13, update_norm)]
    stat_out[...] = stat_tile(pairs)


def final_kernel(parts, loss_scale, all_cells, *refs):
    info_ref, trunk_stat_ref = refs[:2]
    part_refs = refs[2 : 2 + parts]
    enc_ref, enc_update_ref, dec_ref, dec_update_ref, vec_ref, vec_update_ref = refs[2 + parts : 8 + parts]
    loss_out, enc_out, enc_copy, dec_out, dec_copy, vec_out, norm_out = refs[8 + parts :]
    stats = part_refs[0][...]
    for ref in part_refs[1:]:
        stats = stats + ref[...]
    trunk_stats = trunk_stat_ref[...]
    roots = jnp.sqrt(stats[0:1])

    def ratio(index):
        return learn_rate * (roots[:, index : index + 1] / roots[:, index + 4 : index + 5])

    enc_new = enc_ref[...] - ratio(0) * enc_update_ref[...]
    enc_out[...] = enc_new
    enc_copy[...] = enc_new.astype(bf16)
    dec_new = dec_ref[...] - ratio(1) * dec_update_ref[...]
    dec_out[...] = dec_new
    dec_copy[...] = dec_new.astype(bf16)
    vec_ratio = jnp.where(info_ref[0] == 0, ratio(2), ratio(3))
    vec_out[...] = vec_ref[...] - vec_ratio * vec_update_ref[...]
    norm_out[0:1, 0:4] = roots[:, 0:4]
    norm_out[1:2, 0:4] = roots[:, 4:8]
    norm_out[0:1, 4:10] = trunk_stats[0:1, 0:6]
    norm_out[1:2, 4:10] = trunk_stats[0:1, 8:14]
    lane = lax.broadcasted_iota(jnp.int32, (1, 128), 1)
    loss_out[0] = jnp.sum(jnp.where(lane == 8, -stats[0:1], 0.0)) * loss_scale
    loss_out[1] = jnp.sum(jnp.where(lane == 9, stats[0:1], 0.0)) / all_cells


def shaped(*shapes):
    return tuple(jax.ShapeDtypeStruct(shape, kind) for shape, kind in shapes)


def on_device(
    cell_counts,
    cell_seeds,
    batch_ids,
    noise_draw,
    cell_factor,
    enc_weight,
    enc_first,
    enc_second,
    dec_weight,
    dec_first,
    dec_second,
    region_vecs,
    vec_first,
    vec_second,
    trunk_rows,
    trunk_first,
    trunk_second,
    head_rows,
    head_first,
    head_second,
):
    cells_here = cell_counts.shape[0]
    width = enc_weight.shape[0]
    latent = head_rows.shape[1] // 2
    plane = lax.axis_size("plane")
    total = width * COLUMNS * plane
    all_cells = cells_here * lax.axis_size("dp")
    loss_scale = 1.0 / (all_cells * total)
    share = cells_here // COLUMNS
    own = share // plane
    groups = min(4, plane)
    each = plane // groups
    block = own * each
    dp = lax.axis_index("dp")
    column = lax.axis_index("column")
    spot = lax.axis_index("plane")
    info = jnp.stack([dp]).astype(jnp.int32)
    bases = jnp.stack(
        [((column + j) % COLUMNS * plane + spot) * width for j in range(COLUMNS)]
    ).astype(jnp.int32)

    def over_dp(value):
        return lax.ppermute(value, "dp", [(0, 1), (1, 0)])

    def from_column(value, j):
        return lax.ppermute(value, "column", [(i, (i - j) % COLUMNS) for i in range(COLUMNS)])

    def to_column(value, j):
        return lax.ppermute(value, "column", [(i, (i + j) % COLUMNS) for i in range(COLUMNS)])

    def over_plane(value, k):
        return lax.ppermute(value, "plane", [(i, i ^ k) for i in range(plane)])

    def gather_column(value):
        blocks = []
        for j in range(COLUMNS):
            mine = value if j == 0 else from_column(value, j)
            blocks += [mine, over_dp(mine)]
        return blocks

    def gather_plane(value):
        blocks = [value] + [over_plane(value, k) for k in range(1, plane)]
        if each == 1:
            return blocks
        return [jnp.concatenate(blocks[g * each : (g + 1) * each], axis=0) for g in range(groups)]

    def scatter_plane(values):
        received = []
        for g in range(groups):
            for e in range(each):
                k = g * each + e
                piece = values[g] if each == 1 else values[g][e * own : (e + 1) * own]
                received.append(piece if k == 0 else over_plane(piece, k))
        return received

    enc_blocks = gather_column(enc_weight.T.astype(bf16))

    stacked = jnp.stack([cell_counts.astype(f32), cell_seeds.astype(f32), cell_factor])
    stacked = stacked.reshape(3, COLUMNS * plane, own)
    cells = jnp.concatenate(
        [
            lax.dynamic_slice_in_dim(stacked, column * plane + (spot ^ k), 1, axis=1)
            for k in range(plane)
        ],
        axis=1,
    ).reshape(3, share // 128, 128)
    at = (column * plane + spot) * own
    ids = lax.dynamic_slice_in_dim(batch_ids, at, own).reshape(own, 1)
    noise = jnp.pad(lax.dynamic_slice_in_dim(noise_draw, at, own), ((0, 0), (0, 128 - latent)))
    head_wide = jnp.pad(head_rows, ((0, 7), (0, 128 - 2 * latent)))

    regions = COLUMNS * width
    masks, factors = pl.pallas_call(
        functools.partial(mask_kernel, total, width),
        grid=(share // 128,),
        in_specs=[SMEM, pl.BlockSpec(cells.shape, lambda i: (0, 0, 0))],
        out_specs=(
            pl.BlockSpec((128, regions), lambda i: (i, 0)),
            pl.BlockSpec((128, 128), lambda i: (i, 0)),
        ),
        out_shape=shaped(((share, regions), bf16), ((share, 128), f32)),
        compiler_params=params(),
        cost_estimate=cost(6 * share * regions, 2 * share * regions),
        name="masks",
    )(bases, cells)

    def encode(group):
        return pl.pallas_call(
            functools.partial(encode_kernel, width),
            grid=(1,),
            in_specs=[pl.BlockSpec((block, regions), lambda i: (group, 0))]
            + [pl.BlockSpec((64, width), lambda i: (0, 0))] * (2 * COLUMNS),
            out_specs=pl.BlockSpec((block, 128), lambda i: (0, 0)),
            out_shape=jax.ShapeDtypeStruct((block, 128), f32),
            compiler_params=params(),
            cost_estimate=cost(2 * block * regions * 256, 2 * block * regions),
            name="encode",
        )(masks, *enc_blocks)

    partial_pre = [None] * groups
    for g in [*range(1, groups), 0]:
        partial_pre[g] = encode(g)
    pre_parts = scatter_plane(partial_pre)

    dec_send = jnp.concatenate(
        [dec_weight.astype(bf16), region_vecs.astype(bf16), jnp.zeros((15, width), bf16)], axis=0
    )
    dec_send, _ = lax.optimization_barrier((dec_send, partial_pre[1 % groups]))
    dec_blocks = gather_column(dec_send)
    dec_pack, lines = pl.pallas_call(
        pack_kernel,
        in_specs=[SMEM] + [VMEM] * (2 * COLUMNS),
        out_specs=(VMEM, VMEM),
        out_shape=shaped(((COLUMNS, 256, width), bf16), ((COLUMNS, 32, width), f32)),
        compiler_params=params(),
        name="pack",
    )(info, *dec_blocks)

    saved_shapes = shaped(
        ((own, 128), bf16),
        ((4, own, 128), f32),
        ((own, 128), f32),
        ((own, 128), f32),
        ((2, own, 128), f32),
        ((8, 128), f32),
    )
    decoded_low, *saved, trunk_stats = pl.pallas_call(
        functools.partial(forward_kernel, plane, latent, own),
        in_specs=[SMEM] + [VMEM] * (5 + plane),
        out_specs=(VMEM,) * 6,
        out_shape=saved_shapes,
        compiler_params=params(),
        cost_estimate=cost(2 * 30 * own * 128 * 128, 4 * own * 128 * 10),
        name="forward",
    )(info, ids, noise, trunk_rows, head_wide, cells, *pre_parts)

    low_groups = gather_plane(decoded_low)

    def decode(group, low, sums):
        specs = [
            SMEM,
            pl.BlockSpec((block, 128), lambda j: (0, 0)),
            pl.BlockSpec((block, width), lambda j: (group, j)),
            pl.BlockSpec((block, 128), lambda j: (group, 0)),
            pl.BlockSpec((1, 256, width), lambda j: (j, 0, 0)),
            pl.BlockSpec((1, 32, width), lambda j: (j, 0, 0)),
        ]
        sum_spec = pl.BlockSpec((1, 72, width), lambda j: (j, 0, 0))
        return pl.pallas_call(
            functools.partial(decode_kernel, loss_scale, sums is not None),
            grid=(COLUMNS,),
            in_specs=specs + ([] if sums is None else [sum_spec] * 2),
            out_specs=(
                sum_spec,
                sum_spec,
                pl.BlockSpec((block, 128), lambda j: (0, 0)),
                pl.BlockSpec((8, 128), lambda j: (0, 0)),
            ),
            out_shape=shaped(
                ((COLUMNS, 72, width), f32),
                ((COLUMNS, 72, width), f32),
                ((block, 128), f32),
                ((8, 128), f32),
            ),
            scratch_shapes=[
                pltpu.VMEM((block, width), f32),
                pltpu.VMEM((block, width), bf16),
                pltpu.VMEM((block, 256), bf16),
                pltpu.VMEM((144, block), bf16),
            ],
            input_output_aliases={} if sums is None else {6: 0, 7: 1},
            compiler_params=params(),
            cost_estimate=cost(60 * block * regions * 10, 6 * block * regions, 3 * block * regions),
            name="decode",
        )(info, low, masks, factors, dec_pack, lines, *([] if sums is None else sums))

    sums = None
    backs, losses = [], []
    for g in range(groups):
        *sums, back, loss_tile = decode(g, low_groups[g], sums)
        backs.append(back)
        losses.append(loss_tile)
    back_parts = scatter_plane(backs)

    dec_other = over_dp(sums[1])
    dec_parts = [sums[0][0], dec_other[0]]
    for j in range(1, COLUMNS):
        dec_parts.append(to_column(sums[0][j] + dec_other[j], j))

    pre_low, trunk_mine, trunk_other = pl.pallas_call(
        functools.partial(backward_kernel, plane, latent, loss_scale),
        in_specs=[SMEM] + [VMEM] * (8 + plane),
        out_specs=(VMEM,) * 3,
        out_shape=shaped(((own, 128), bf16), ((160, 128), f32), ((160, 128), f32)),
        scratch_shapes=[pltpu.VMEM((320, 128), f32)],
        compiler_params=params(),
        cost_estimate=cost(2 * 60 * own * 128 * 128, 4 * own * 128 * 10),
        name="backward",
    )(info, ids, noise, trunk_rows, head_wide, *saved, *back_parts)

    pre_groups = gather_plane(pre_low)
    enc_sums = pl.pallas_call(
        functools.partial(encode_back_kernel, groups),
        grid=(COLUMNS,),
        in_specs=[pl.BlockSpec((share, width), lambda j: (0, j))]
        + [pl.BlockSpec((block, 128), lambda j: (0, 0))] * groups,
        out_specs=(pl.BlockSpec((1, 64, width), lambda j: (j, 0, 0)),) * 2,
        out_shape=shaped(((COLUMNS, 64, width), f32), ((COLUMNS, 64, width), f32)),
        scratch_shapes=[pltpu.VMEM((128, share), bf16)],
        compiler_params=params(),
        cost_estimate=cost(2 * share * regions * 256, 2 * share * regions),
        name="encode_back",
    )(masks, *pre_groups)
    enc_other = over_dp(enc_sums[1])
    enc_parts = [enc_sums[0][0], enc_other[0]]
    for j in range(1, COLUMNS):
        enc_parts.append(to_column(enc_sums[0][j] + enc_other[j], j))

    trunk_half = trunk_mine + over_dp(trunk_other)
    trunk_half = trunk_half + sum(from_column(trunk_half, j) for j in range(1, COLUMNS))
    trunk_half = trunk_half + sum(over_plane(trunk_half, k) for k in range(1, plane))
    trunk_rest = over_dp(trunk_half)

    like = lambda *arrays: shaped(*((x.shape, f32) for x in arrays))
    tile = jax.ShapeDtypeStruct((8, 128), f32)
    dec_first_new, dec_second_new, dec_update, vec_first_new, vec_second_new, vec_update, dec_stats = (
        pl.pallas_call(
            functools.partial(dec_lamb_kernel, len(dec_parts), loss_scale),
            in_specs=[SMEM] + [VMEM] * (6 + len(dec_parts)),
            out_specs=(VMEM,) * 7,
            out_shape=like(dec_weight, dec_weight, dec_weight, region_vecs, region_vecs, region_vecs)
            + (tile,),
            compiler_params=params(),
            name="dec_lamb",
        )(info, dec_weight, dec_first, dec_second, region_vecs, vec_first, vec_second, *dec_parts)
    )
    (
        trunk_new,
        trunk_first_new,
        trunk_second_new,
        head_new,
        head_first_new,
        head_second_new,
        trunk_norms,
    ) = pl.pallas_call(
        functools.partial(trunk_lamb_kernel, latent),
        in_specs=[SMEM] + [VMEM] * 8,
        out_specs=(VMEM,) * 7,
        out_shape=like(trunk_rows, trunk_rows, trunk_rows, head_rows, head_rows, head_rows) + (tile,),
        scratch_shapes=[pltpu.VMEM((320, 128), f32)],
        compiler_params=params(),
        name="trunk_lamb",
    )(
        info,
        trunk_half,
        trunk_rest,
        trunk_rows,
        trunk_first,
        trunk_second,
        head_rows,
        head_first,
        head_second,
    )
    enc_first_new, enc_second_new, enc_update, enc_stats = pl.pallas_call(
        functools.partial(enc_lamb_kernel, len(enc_parts)),
        in_specs=[VMEM] * (3 + len(enc_parts)),
        out_specs=(VMEM,) * 4,
        out_shape=like(enc_weight, enc_weight, enc_weight) + (tile,),
        compiler_params=params(),
        name="enc_lamb",
    )(enc_weight, enc_first, enc_second, *enc_parts)

    lane = lax.broadcasted_iota(jnp.int32, (8, 128), 1)
    row = lax.broadcasted_iota(jnp.int32, (8, 128), 0)
    loss_sum = jnp.sum(sum(losses))
    stats = enc_stats + dec_stats + trunk_stats
    stats = stats + jnp.where((lane == 8) & (row == 0), loss_sum, 0.0)
    stats = stats + over_dp(stats)
    stats = stats + sum(over_plane(stats, k) for k in range(1, plane))
    stat_parts = [stats] + [from_column(stats, j) for j in range(1, COLUMNS)]
    loss, enc_new, enc_copy, dec_new, dec_copy, vecs_new, norms = pl.pallas_call(
        functools.partial(final_kernel, len(stat_parts), loss_scale, all_cells),
        in_specs=[SMEM] + [VMEM] * (7 + len(stat_parts)),
        out_specs=(SMEM,) + (VMEM,) * 6,
        out_shape=shaped(
            ((2,), f32),
            (enc_weight.shape, f32),
            (enc_weight.shape, bf16),
            (dec_weight.shape, f32),
            (dec_weight.shape, bf16),
            (region_vecs.shape, f32),
            ((2, 10), f32),
        ),
        compiler_params=params(),
        name="final",
    )(
        info,
        trunk_norms,
        *stat_parts,
        enc_weight,
        enc_update,
        dec_weight,
        dec_update,
        region_vecs,
        vec_update,
    )
    return (
        loss,
        enc_new,
        enc_first_new,
        enc_second_new,
        enc_copy,
        dec_new,
        dec_first_new,
        dec_second_new,
        dec_copy,
        vecs_new,
        vec_first_new,
        vec_second_new,
        trunk_new,
        trunk_first_new,
        trunk_second_new,
        head_new,
        head_first_new,
        head_second_new,
        norms,
    )


def solution(mesh):
    regions = mesh.shape["region"]
    devices = mesh.devices.reshape(mesh.shape["dp"], COLUMNS, regions // COLUMNS)
    inner = Mesh(devices, ("dp", "column", "plane"))
    across = ("column", "plane")
    by_row, by_line = P(across, "dp"), P("dp", across)
    return jax.shard_map(
        on_device,
        mesh=inner,
        in_specs=(P("dp"), P("dp"), P("dp"), P("dp", None), P("dp"))
        + (by_row,) * 3
        + (by_line,) * 6
        + (P(),) * 6,
        out_specs=(P(),) + (by_row,) * 4 + (by_line,) * 7 + (P(),) * 7,
        check_vma=False,
    )
```

time: 888 us -> 243 us (0.27); the launches traced: 878 us -> 242 us
  matrix products: 299 us -> 0 us
  waiting for transfers between devices: 301 us -> 51.4 us
  Pallas kernels: 0 us -> 106 us
  blocking collectives: 93.3 us -> 0 us
  other arithmetic: 95.9 us -> 8.65 us
  starting transfers between devices: 0.2 us -> 52 us
  between operations: 31.4 us -> 1.16 us
  local copies, waits for them, and re-layouts: 50 us -> 22.1 us
    dot_general x56 -> x0, matrix products: 299 us -> none  [the longest x15 97.4 us: matmul(): jnp.dot(left, right, precision=highest, preferred_element_type=jnp.float32)]
    psum x3 -> x0, waiting for transfers between devices: 297 us -> none  [the longest x1 165 us: on_device(): enc_total = lax.psum(partial_pre, 'region')]
    pallas_call x0 -> x17, Pallas kernels: none -> 106 us  [the longest x4 59.7 us: decode(): pl.pallas_call(functools.partial(decode_kernel, loss_scale, sums is not N...]
    psum x3 -> x0, blocking collectives: 87.5 us -> none  [the longest x1 42.5 us: on_device(): hidden_grad, recon_region = lax.psum((back_hidden, recon_sum), 'region')]
    reduce_sum x28 -> x1, other arithmetic: 62.3 us -> 0.6 us  [on_device(): loss_sum = jnp.sum(sum(losses))]
    ppermute x0 -> x49, starting transfers between devices: none -> 52 us  [the longest x18 21.2 us: over_plane(): return lax.ppermute(value, 'plane', [(i, i ^ k) for i in range(plane)])]
    ppermute x0 -> x49, waiting for transfers between devices: none -> 51.4 us  [the longest x18 18.9 us: over_plane(): return lax.ppermute(value, 'plane', [(i, i ^ k) for i in range(plane)])]
    dynamic_slice x24 -> x3, local copies, waits for them, and re-layouts: 18.9 us -> 0.79 us  [the longest x1 0.76 us: on_device(): ids = lax.dynamic_slice_in_dim(batch_ids, at, own).reshape(own, 1)]
  transfers between devices with their start and end apart: 5 -> 49, of which waited for: 4 -> 15; matrix products, arithmetic and copies ran while one was open for 2% -> 9% of each run, Pallas kernels for 0% -> 34%
where the time goes in v1:
time: 243 us; the launch traced here: 242 us
  Pallas kernels  106 us (44%)
  starting transfers between devices  52 us (21%)
  waiting for transfers between devices  51.4 us (21%)
  local copies, waits for them, and re-layouts  22.1 us (9%)
  other arithmetic  8.65 us (4%)
    pallas_call x4, Pallas kernels, decode(): pl.pallas_call(functools.partial(decode_kernel, loss_scale, sums is not N...  59.7 us
    ppermute x18, starting transfers between devices, over_plane(): return lax.ppermute(value, 'plane', [(i, i ^ k) for i in range(plane)])  21.2 us
    ppermute x12, starting transfers between devices, from_column(): lax.ppermute(value, 'column', [(i, (i - j) % COLUMNS) for i in range(COLU...  20.2 us
    unnamed x56, local copies, waits for them, and re-layouts  19.3 us
    ppermute x18, waiting for transfers between devices, over_plane(): return lax.ppermute(value, 'plane', [(i, i ^ k) for i in range(plane)])  18.9 us
    ppermute x12, waiting for transfers between devices, from_column(): lax.ppermute(value, 'column', [(i, (i - j) % COLUMNS) for i in range(COLU...  18.9 us
    pallas_call x1, Pallas kernels, on_device(): pl.pallas_call(functools.partial(mask_kernel, total, width), grid=(share...  13.6 us
    pallas_call x4, Pallas kernels, encode(): pl.pallas_call(functools.partial(encode_kernel, width), grid=(1,), in_spe...  12.9 us
  transfers between devices with their start and end apart: 49, of which 15 were waited for; matrix products, arithmetic and copies ran while one was open for 9% of the time, Pallas kernels for 34%

profile of v1, /device:TPU:0, one launch (start us, length us, event | category | flops | bytes accessed | tf_op | source)
XLA Modules:
  0.0 241.6 jit_solution(14027152415008231612)
XLA Ops:
  0.7 1.0 convert_bitcast_fusion.refs_0_
  1.7 5.1 %collective-permute-start.1 = (bf16[64,768]{1,0:T(8,128)(2,1)S(1)}, bf16[64,768]{1,0:T(8,128)(2,1)S(1)}, u32[]{:S(2)}, u32[]{:S(2)}) collective-permute-start(bf16[64,768]{1,0:T(8,128)(2,1)S(1)} %convert_bitcast_fusion.refs_0_), channel_id=1, source_target_pairs={{0,12},{4,0},{8,4},{12,8},{1,13},{5,1},{9,5},{13,9},{2,14},{6,2},{... | collective-permute-start | bytes 294920 | tf_op jit(solution)/shard_map/ppermute | solution.py:565
  6.8 1.0 collective-permute-start.5
  10.1 0.9 convert_element_type.25
  12.7 2.9 %collective-permute-done.3.refs_4_ = bf16[64,768]{1,0:T(8,128)(2,1)S(1)} collective-permute-done((bf16[64,768]{1,0:T(8,128)(2,1)S(1)}, bf16[64,768]{1,0:T(8,128)(2,1)S(1)}, u32[]{:S(2)}, u32[]{:S(2)}) %collective-permute-start.3) | collective-permute-done | bytes 98336 | tf_op jit(solution)/shard_map/ppermute | solution.py:565
  16.1 13.6 %masks.1 = (bf16[2048,3072]{1,0:T(8,128)(2,1)}, f32[2048,128]{1,0:T(8,128)S(1)}) custom-call(s32[4]{0:T(128)S(1)} %pad_add_fusion.base_ref, f32[3,16,128]{2,1,0:T(8,128)S(1)} %reshape.58.cells_ref.refs_5_), custom_call_target="tpu_custom_call" | custom-call | flops 37748736 | bytes 12582912 | tf_op jit(solution)/shard_map/masks/pallas_call | solution.py:612
  29.8 3.6 %encode.7 = f32[512,128]{1,0:T(8,128)} custom-call(bf16[2048,3072]{1,0:T(8,128)(2,1)} %get-tuple-element.76.mask_ref.refs_2_, bf16[64,768]{1,0:T(8,128)(2,1)S(1)} %convert_bitcast_fusion.refs_0_, bf16[64,768]{1,0:T(8,128)(2,1)S(1)} %collective-permute-done.refs_1_, bf16[64,768]{1,0:T(8,128)(2,1)S(1)} %collective-permute-done.1.refs_2_, ...), custom_call_target="tpu_custom_call" | custom-call | flops 805306368 | bytes 3145728 | tf_op jit(solution)/shard_map/encode/pallas_call | solution.py:627
  33.3 2.4 %collective-permute-start.9 = (f32[512,128]{1,0:T(8,128)}, f32[512,128]{1,0:T(8,128)}, u32[]{:S(2)}, u32[]{:S(2)}) collective-permute-start(f32[512,128]{1,0:T(8,128)} %encode.7), channel_id=1, source_target_pairs={{0,3},{1,2},{2,1},{3,0},{4,7},{5,6},{6,5},{7,4},{8,11},{9,10},{10,... | collective-permute-start | bytes 786440 | tf_op jit(solution)/shard_map/ppermute | solution.py:571
  35.8 3.6 %encode.6 = f32[512,128]{1,0:T(8,128)} custom-call(bf16[2048,3072]{1,0:T(8,128)(2,1)} %get-tuple-element.76.mask_ref.refs_2_, bf16[64,768]{1,0:T(8,128)(2,1)S(1)} %convert_bitcast_fusion.refs_0_, bf16[64,768]{1,0:T(8,128)(2,1)S(1)} %collective-permute-done.refs_1_, bf16[64,768]{1,0:T(8,128)(2,1)S(1)} %collective-permute-done.1.refs_2_, ...), custom_call_target="tpu_custom_call" | custom-call | flops 805306368 | bytes 3145728 | tf_op jit(solution)/shard_map/encode/pallas_call | solution.py:627
  39.9 2.9 %encode.5 = f32[512,128]{1,0:T(8,128)S(1)} custom-call(bf16[2048,3072]{1,0:T(8,128)(2,1)} %get-tuple-element.76.mask_ref.refs_2_, bf16[64,768]{1,0:T(8,128)(2,1)S(1)} %convert_bitcast_fusion.refs_0_, bf16[64,768]{1,0:T(8,128)(2,1)S(1)} %collective-permute-done.refs_1_, bf16[64,768]{1,0:T(8,128)(2,1)S(1)} %collective-permute-done.1.refs_2_, ...), custom_call_target="tpu_custom_call" | custom-call | flops 805306368 | bytes 3145728 | tf_op jit(solution)/shard_map/encode/pallas_call | solution.py:627
  42.7 2.0 collective-permute-start.11
  45.3 3.0 %collective-permute-done.11.refs_2_ = bf16[80,768]{1,0:T(8,128)(2,1)S(1)} collective-permute-done((bf16[80,768]{1,0:T(8,128)(2,1)S(1)}, bf16[80,768]{1,0:T(8,128)(2,1)S(1)}, u32[]{:S(2)}, u32[]{:S(2)}) %collective-permute-start.11) | collective-permute-done | bytes 122912 | tf_op jit(solution)/shard_map/ppermute | solution.py:565
  51.6 1.0 pad.8.refs_2_
  52.6 3.3 %collective-permute-done.13.refs_4_ = bf16[80,768]{1,0:T(8,128)(2,1)S(1)} collective-permute-done((bf16[80,768]{1,0:T(8,128)(2,1)S(1)}, bf16[80,768]{1,0:T(8,128)(2,1)S(1)}, u32[]{:S(2)}, u32[]{:S(2)}) %collective-permute-start.13) | collective-permute-done | bytes 122912 | tf_op jit(solution)/shard_map/ppermute | solution.py:565
  56.9 2.9 %encode.4.refs_6_ = f32[512,128]{1,0:T(8,128)S(1)} custom-call(bf16[2048,3072]{1,0:T(8,128)(2,1)} %get-tuple-element.76.mask_ref.refs_2_, bf16[64,768]{1,0:T(8,128)(2,1)S(1)} %convert_bitcast_fusion.refs_0_, bf16[64,768]{1,0:T(8,128)(2,1)S(1)} %collective-permute-done.refs_1_, bf16[64,768]{1,0:T(8,128)(2,1)S(1)} %collective-permute-done.1.refs_2_, ...), custom_call_target="tpu_custom_call" | custom-call | flops 805306368 | bytes 3145728 | tf_op jit(solution)/shard_map/encode/pallas_call | solution.py:627
  59.8 4.6 %forward.1 = (bf16[512,128]{1,0:T(8,128)(2,1)S(1)}, f32[4,512,128]{2,1,0:T(8,128)S(1)}, f32[512,128]{1,0:T(8,128)S(1)}, f32[512,128]{1,0:T(8,128)S(1)}, f32[2,51...) custom-call(s32[1]{0:T(128)} %bitcast.refs_0_.info_ref, s32[512,1]{1,0:T(8,128)S(1)} %copy.64.refs_1_, ...), custom_call_target="tpu_custom_call" | custom-call | flops 503316480 | bytes 2621440 | tf_op jit(solution)/shard_map/forward/pallas_call | solution.py:666
  64.4 1.0 collective-permute-start.17
  65.4 1.1 pack.1
  66.5 1.6 collective-permute-start.19
  68.1 1.0 collective-permute-start.21
  69.1 14.9 %decode.4 = (f32[4,72,768]{2,1,0:T(8,128)S(1)}, f32[4,72,768]{2,1,0:T(8,128)S(1)}, f32[512,128]{1,0:T(8,128)S(1)}, f32[8,128]{1,0:T(8,128)S(1)}) custom-call(s32[1]{0:T(128)} %bitcast.refs_0_.info_ref, bf16[512,128]{1,0:T(8,128)(2,1)S(1)} %get-tuple-element.81.refs_1_, bf16[2048,3072]{1,0:T(8,128)(2,1)} %get-tuple-element.76.mask_ref.refs_2_, ...), custom_call_target="tpu_custom_call" | custom-call | flops 943718400 | bytes 9437184 | tf_op jit(solution)/shard_map/decode/pallas_call | solution.py:688
  84.0 14.9 %decode.5 = (f32[4,72,768]{2,1,0:T(8,128)S(1)}, f32[4,72,768]{2,1,0:T(8,128)S(1)}, f32[512,128]{1,0:T(8,128)S(1)}, f32[8,128]{1,0:T(8,128)S(1)}) custom-call(s32[1]{0:T(128)} %bitcast.refs_0_.info_ref, bf16[512,128]{1,0:T(8,128)(2,1)S(1)} %collective-permute-done.17.refs_1_, ...), custom_call_target="tpu_custom_call", output_to_operand_aliasing={{0}: (6, {}), {1}: (7, {})} | custom-call | flops 943718400 | bytes 9437184 | tf_op jit(solution)/shard_map/decode/pallas_call | solution.py:688
  98.9 14.9 %decode.6 = (f32[4,72,768]{2,1,0:T(8,128)S(1)}, f32[4,72,768]{2,1,0:T(8,128)S(1)}, f32[512,128]{1,0:T(8,128)S(1)}, f32[8,128]{1,0:T(8,128)S(1)}) custom-call(s32[1]{0:T(128)} %bitcast.refs_0_.info_ref, bf16[512,128]{1,0:T(8,128)(2,1)S(1)} %collective-permute-done.19.refs_1_, ...), custom_call_target="tpu_custom_call", output_to_operand_aliasing={{0}: (6, {}), {1}: (7, {})} | custom-call | flops 943718400 | bytes 9437184 | tf_op jit(solution)/shard_map/decode/pallas_call | solution.py:688
  113.9 15.0 %decode.7 = (f32[4,72,768]{2,1,0:T(8,128)S(1)}, f32[4,72,768]{2,1,0:T(8,128)S(1)}, f32[512,128]{1,0:T(8,128)S(1)}, f32[8,128]{1,0:T(8,128)S(1)}) custom-call(s32[1]{0:T(128)} %bitcast.refs_0_.info_ref, bf16[512,128]{1,0:T(8,128)(2,1)S(1)} %collective-permute-done.21.refs_1_, ...), custom_call_target="tpu_custom_call", output_to_operand_aliasing={{0}: (6, {}), {1}: (7, {})} | custom-call | flops 943718400 | bytes 9437184 | tf_op jit(solution)/shard_map/decode/pallas_call | solution.py:688
  129.0 1.9 collective-permute-start.22
  131.4 1.1 collective-permute-start.18
  132.5 6.7 %collective-permute-done.22.refs_12_ = f32[512,128]{1,0:T(8,128)S(1)} collective-permute-done((f32[512,128]{1,0:T(8,128)S(1)}, f32[512,128]{1,0:T(8,128)S(1)}, u32[]{:S(2)}, u32[]{:S(2)}) %collective-permute-start.22) | collective-permute-done | bytes 262176 | tf_op jit(solution)/shard_map/ppermute | solution.py:571
  139.2 3.8 %collective-permute-done.20.refs_11_ = f32[512,128]{1,0:T(8,128)S(1)} collective-permute-done((f32[512,128]{1,0:T(8,128)S(1)}, f32[512,128]{1,0:T(8,128)S(1)}, u32[]{:S(2)}, u32[]{:S(2)}) %collective-permute-start.20) | collective-permute-done | bytes 262176 | tf_op jit(solution)/shard_map/ppermute | solution.py:571
  143.1 3.9 %backward.1 = (bf16[512,128]{1,0:T(8,128)(2,1)S(1)}, f32[160,128]{1,0:T(8,128)S(1)}, f32[160,128]{1,0:T(8,128)S(1)}) custom-call(s32[1]{0:T(128)} %bitcast.refs_0_.info_ref, s32[512,1]{1,0:T(8,128)S(1)} %copy-done.4, f32[512,128]{1,0:T(8,128)S(1)} %pad.8.refs_2_, f32[290,128]{1,0:T(8,128)S(1)} %copy-done.7, f32[136,128]{1,0:T(8,128)S(1)} %pad.9.refs_4_, ...), custom_call_target="tpu_custom_call" | custom-call | flops 1006632960 | bytes 2621440 | tf_op jit(solution)/shard_map/backward/pallas_call | solution.py:729
  147.0 1.0 collective-permute-start.31
  148.0 1.3 collective-permute-start.32
  149.2 1.3 collective-permute-start.33
  150.5 2.8 %collective-permute-done.31.refs_1_ = bf16[512,128]{1,0:T(8,128)(2,1)S(1)} collective-permute-done((bf16[512,128]{1,0:T(8,128)(2,1)S(1)}, bf16[512,128]{1,0:T(8,128)(2,1)S(1)}, u32[]{:S(2)}, u32[]{:S(2)}) %collective-permute-start.31) | collective-permute-done | bytes 131104 | tf_op jit(solution)/shard_map/ppermute | solution.py:571
  153.4 2.4 %collective-permute-done.32.refs_2_ = bf16[512,128]{1,0:T(8,128)(2,1)S(1)} collective-permute-done((bf16[512,128]{1,0:T(8,128)(2,1)S(1)}, bf16[512,128]{1,0:T(8,128)(2,1)S(1)}, u32[]{:S(2)}, u32[]{:S(2)}) %collective-permute-start.32) | collective-permute-done | bytes 131104 | tf_op jit(solution)/shard_map/ppermute | solution.py:571
  155.8 7.0 %encode_back.1 = (f32[4,64,768]{2,1,0:T(8,128)S(1)}, f32[4,64,768]{2,1,0:T(8,128)}) custom-call(bf16[2048,3072]{1,0:T(8,128)(2,1)} %get-tuple-element.76.mask_ref.refs_2_, bf16[512,128]{1,0:T(8,128)(2,1)S(1)} %get-tuple-element.99.refs_0_, bf16[512,128]{1,0:T(8,128)(2,1)S(1)} %collective-permute-done.31.refs_1_, ...), custom_call_target="tpu_custom_call" | custom-call | flops 3221225472 | bytes 12582912 | tf_op jit(solution)/shard_map/encode_back/pallas_call | solution.py:741
  163.9 1.1 copy.69.refs_1_
  165.0 1.9 copy.70.refs_2_
  168.6 1.8 collective-permute-start.24
  170.9 1.9 collective-permute-start.26
  172.9 1.4 fusion
  174.2 1.1 collective-permute-start.39
  175.3 1.4 collective-permute-start.40
  176.7 1.5 fusion.3
  178.3 1.4 collective-permute-start.41
  179.7 9.7 %collective-permute-done.25 = f32[160,128]{1,0:T(8,128)S(1)} collective-permute-done((f32[160,128]{1,0:T(8,128)S(1)}, f32[160,128]{1,0:T(8,128)S(1)}, u32[]{:S(2)}, u32[]{:S(2)}) %collective-permute-start.25) | collective-permute-done | bytes 81952 | tf_op jit(solution)/shard_map/ppermute | solution.py:565
  189.4 3.9 %collective-permute-start.37 = (f32[64,768]{1,0:T(8,128)S(1)}, f32[64,768]{1,0:T(8,128)S(1)}, u32[]{:S(2)}, u32[]{:S(2)}) collective-permute-start(f32[64,768]{1,0:T(8,128)S(1)} %get-tuple-element.174), channel_id=1, source_target_pairs={{0,12},{4,0},{8,4},{12,8},{1,13},{5,1},{9,5},{13,9},{2,14},{6,2},{... | collective-permute-start | bytes 589832 | tf_op jit(solution)/shard_map/ppermute | solution.py:568
  193.3 8.5 %collective-permute-done.40.refs_10_ = f32[72,768]{1,0:T(8,128)S(1)} collective-permute-done((f32[72,768]{1,0:T(8,128)S(1)}, f32[72,768]{1,0:T(8,128)S(1)}, u32[]{:S(2)}, u32[]{:S(2)}) %collective-permute-start.40) | collective-permute-done | bytes 221216 | tf_op jit(solution)/shard_map/ppermute | solution.py:568
  201.9 1.3 collective-permute-start.27
  204.0 0.9 copy-done.9
  204.9 0.9 copy-done.10
  205.9 0.9 dec_lamb.1
  206.8 1.4 collective-permute-start.29
  208.2 3.4 %collective-permute-done.36.refs_6_ = f32[64,768]{1,0:T(8,128)S(1)} collective-permute-done((f32[64,768]{1,0:T(8,128)S(1)}, f32[64,768]{1,0:T(8,128)S(1)}, u32[]{:S(2)}, u32[]{:S(2)}) %collective-permute-start.36) | collective-permute-done | bytes 196640 | tf_op jit(solution)/shard_map/ppermute | solution.py:568
  211.5 1.0 copy-done.2
  213.8 1.2 collective-permute-done.42
  215.0 1.3 collective-permute-start.43
  217.1 1.3 collective-permute-start.45
  218.6 1.3 collective-permute-done.44
  219.8 1.8 collective-permute-done.45
  221.6 6.5 %collective-permute-start.46 = (f32[8,128]{1,0:T(8,128)S(1)}, f32[8,128]{1,0:T(8,128)S(1)}, u32[]{:S(2)}, u32[]{:S(2)}) collective-permute-start(f32[8,128]{1,0:T(8,128)S(1)} %add_add_fusion.2.refs_2_), channel_id=1, source_target_pairs={{0,12},{4,0},{8,4},{12,8},{1,13},{5,1},{9,5},{13,9},{2,14},{6,2},{... | collective-permute-start | bytes 12296 | tf_op jit(solution)/shard_map/ppermute | solution.py:565
  231.4 0.9 copy-done.13
  233.2 1.1 trunk_lamb.1
  238.1 0.9 copy-done.12
  239.0 1.0 final.1
  (139 shorter events, 26.4 us)
Async XLA Ops:
  0.7 48.3 %copy-start = (f32[8192,10]{0,1:T(8,128)S(1)}, f32[8192,10]{0,1:T(8,128)}, u32[]{:S(2)}) copy-start(f32[8192,10]{0,1:T(8,128)} %param.23) | copy-start | bytes 983044
  1.7 10.4 %collective-permute-start.1 = (bf16[64,768]{1,0:T(8,128)(2,1)S(1)}, bf16[64,768]{1,0:T(8,128)(2,1)S(1)}, u32[]{:S(2)}, u32[]{:S(2)}) collective-permute-start(bf16[64,768]{1,0:T(8,128)(2,1)S(1)} %convert_bitcast_fusion.refs_0_), channel_id=1, source_target_pairs={{0,12},{4,0},{8,4},{12,8},{1,13},{5,1},{9,5},{13,9},{2,14},{6,2},{... | collective-permute-start | bytes 294920 | tf_op jit(solution)/shard_map/ppermute | solution.py:565
  6.8 8.7 %collective-permute-start.3 = (bf16[64,768]{1,0:T(8,128)(2,1)S(1)}, bf16[64,768]{1,0:T(8,128)(2,1)S(1)}, u32[]{:S(2)}, u32[]{:S(2)}) collective-permute-start(bf16[64,768]{1,0:T(8,128)(2,1)S(1)} %convert_bitcast_fusion.refs_0_), channel_id=1, source_target_pairs={{0,8},{4,12},{8,0},{12,4},{1,9},{5,13},{9,1},{13,5},{2,10},{6,14},... | collective-permute-start | bytes 294920 | tf_op jit(solution)/shard_map/ppermute | solution.py:565
  6.8 8.8 %collective-permute-start.5 = (bf16[64,768]{1,0:T(8,128)(2,1)S(1)}, bf16[64,768]{1,0:T(8,128)(2,1)S(1)}, u32[]{:S(2)}, u32[]{:S(2)}) collective-permute-start(bf16[64,768]{1,0:T(8,128)(2,1)S(1)} %convert_bitcast_fusion.refs_0_), channel_id=1, source_target_pairs={{0,4},{4,8},{8,12},{12,0},{1,5},{5,9},{9,13},{13,1},{2,6},{6,10},{... | collective-permute-start | bytes 294920 | tf_op jit(solution)/shard_map/ppermute | solution.py:565
  7.8 22.0 %collective-permute-start = (bf16[64,768]{1,0:T(8,128)(2,1)S(1)}, bf16[64,768]{1,0:T(8,128)(2,1)S(1)}, u32[]{:S(2)}, u32[]{:S(2)}) collective-permute-start(bf16[64,768]{1,0:T(8,128)(2,1)S(1)} %convert_bitcast_fusion.refs_0_), channel_id=1, source_target_pairs={{0,16},{16,0},{1,17},{17,1},{2,18},{18,2},{3,19},{19,3},{4,20},{20... | collective-permute-start | bytes 294920 | tf_op jit(solution)/shard_map/ppermute | solution.py:562
  12.1 17.7 %collective-permute-start.2 = (bf16[64,768]{1,0:T(8,128)(2,1)S(1)}, bf16[64,768]{1,0:T(8,128)(2,1)S(1)}, u32[]{:S(2)}, u32[]{:S(2)}) collective-permute-start(bf16[64,768]{1,0:T(8,128)(2,1)S(1)} %collective-permute-done.1.refs_2_), channel_id=1, source_target_pairs={{0,16},{16,0},{1,17},{17,1},{2,18},{18,2},{3,19},{19,3},{4,20},{20... | collective-permute-start | bytes 294920 | tf_op jit(solution)/shard_map/ppermute | solution.py:562
  15.5 14.2 %collective-permute-start.4 = (bf16[64,768]{1,0:T(8,128)(2,1)S(1)}, bf16[64,768]{1,0:T(8,128)(2,1)S(1)}, u32[]{:S(2)}, u32[]{:S(2)}) collective-permute-start(bf16[64,768]{1,0:T(8,128)(2,1)S(1)} %collective-permute-done.3.refs_4_), channel_id=1, source_target_pairs={{0,16},{16,0},{1,17},{17,1},{2,18},{18,2},{3,19},{19,3},{4,20},{20... | collective-permute-start | bytes 294920 | tf_op jit(solution)/shard_map/ppermute | solution.py:562
  15.5 14.2 %collective-permute-start.6 = (bf16[64,768]{1,0:T(8,128)(2,1)S(1)}, bf16[64,768]{1,0:T(8,128)(2,1)S(1)}, u32[]{:S(2)}, u32[]{:S(2)}) collective-permute-start(bf16[64,768]{1,0:T(8,128)(2,1)S(1)} %collective-permute-done.5.refs_6_), channel_id=1, source_target_pairs={{0,16},{16,0},{1,17},{17,1},{2,18},{18,2},{3,19},{19,3},{4,20},{20... | collective-permute-start | bytes 294920 | tf_op jit(solution)/shard_map/ppermute | solution.py:562
  33.3 23.1 %collective-permute-start.9 = (f32[512,128]{1,0:T(8,128)}, f32[512,128]{1,0:T(8,128)}, u32[]{:S(2)}, u32[]{:S(2)}) collective-permute-start(f32[512,128]{1,0:T(8,128)} %encode.7), channel_id=1, source_target_pairs={{0,3},{1,2},{2,1},{3,0},{4,7},{5,6},{6,5},{7,4},{8,11},{9,10},{10,... | collective-permute-start | bytes 786440 | tf_op jit(solution)/shard_map/ppermute | solution.py:571
  39.4 20.4 %copy-start.6 = (f32[290,128]{1,0:T(8,128)S(1)}, f32[290,128]{1,0:T(8,128)}, u32[]{:S(2)}) copy-start(f32[290,128]{1,0:T(8,128)} %refs_3_.6) | copy-start | bytes 445444
  39.4 17.1 %collective-permute-start.8 = (f32[512,128]{1,0:T(8,128)}, f32[512,128]{1,0:T(8,128)}, u32[]{:S(2)}, u32[]{:S(2)}) collective-permute-start(f32[512,128]{1,0:T(8,128)} %encode.6), channel_id=1, source_target_pairs={{0,2},{1,3},{2,0},{3,1},{4,6},{5,7},{6,4},{7,5},{8,10},{9,11},{10,... | collective-permute-start | bytes 786440 | tf_op jit(solution)/shard_map/ppermute | solution.py:571
  42.7 5.5 %collective-permute-start.11 = (bf16[80,768]{1,0:T(8,128)(2,1)S(1)}, bf16[80,768]{1,0:T(8,128)(2,1)S(1)}, u32[]{:S(2)}, u32[]{:S(2)}) collective-permute-start(bf16[80,768]{1,0:T(8,128)(2,1)S(1)} %maximum_maximum_fusion.refs_0_), channel_id=1, source_target_pairs={{0,12},{4,0},{8,4},{12,8},{1,13},{5,1},{9,5},{13,9},{2,14},{6,2},{... | collective-permute-start | bytes 368648 | tf_op jit(solution)/shard_map/ppermute | solution.py:565
  44.7 15.1 %collective-permute-start.7 = (f32[512,128]{1,0:T(8,128)S(1)}, f32[512,128]{1,0:T(8,128)}, u32[]{:S(2)}, u32[]{:S(2)}) collective-permute-start(f32[512,128]{1,0:T(8,128)S(1)} %encode.5), channel_id=1, source_target_pairs={{0,1},{1,0},{2,3},{3,2},{4,5},{5,4},{6,7},{7,6},{8,9},{9,8},{10,11... | collective-permute-start | bytes 786440 | tf_op jit(solution)/shard_map/ppermute | solution.py:571
  45.3 10.6 %collective-permute-start.13 = (bf16[80,768]{1,0:T(8,128)(2,1)S(1)}, bf16[80,768]{1,0:T(8,128)(2,1)S(1)}, u32[]{:S(2)}, u32[]{:S(2)}) collective-permute-start(bf16[80,768]{1,0:T(8,128)(2,1)S(1)} %maximum_maximum_fusion.refs_0_), channel_id=1, source_target_pairs={{0,8},{4,12},{8,0},{12,4},{1,9},{5,13},{9,1},{13,5},{2,10},{6,14},... | collective-permute-start | bytes 368648 | tf_op jit(solution)/shard_map/ppermute | solution.py:565
  48.3 7.6 %collective-permute-start.15 = (bf16[80,768]{1,0:T(8,128)(2,1)S(1)}, bf16[80,768]{1,0:T(8,128)(2,1)}, u32[]{:S(2)}, u32[]{:S(2)}) collective-permute-start(bf16[80,768]{1,0:T(8,128)(2,1)S(1)} %maximum_maximum_fusion.refs_0_), channel_id=1, source_target_pairs={{0,4},{4,8},{8,12},{12,0},{1,5},{5,9},{9,13},{13,1},{2,6},{6,10},{... | collective-permute-start | bytes 368648 | tf_op jit(solution)/shard_map/ppermute | solution.py:565
  50.7 18.4 %copy-start.3 = (s32[512,1]{1,0:T(8,128)}, s32[512,1]{1,0:T(8,128)S(1)}, u32[]{:S(2)}) copy-start(s32[512,1]{1,0:T(8,128)S(1)} %copy.64.refs_1_) | copy-start | bytes 6148
  55.9 9.5 %collective-permute-start.10 = (bf16[80,768]{1,0:T(8,128)(2,1)S(1)}, bf16[80,768]{1,0:T(8,128)(2,1)S(1)}, u32[]{:S(2)}, u32[]{:S(2)}) collective-permute-start(bf16[80,768]{1,0:T(8,128)(2,1)S(1)} %maximum_maximum_fusion.refs_0_), channel_id=1, source_target_pairs={{0,16},{16,0},{1,17},{17,1},{2,18},{18,2},{3,19},{19,3},{4,20},{20... | collective-permute-start | bytes 368648 | tf_op jit(solution)/shard_map/ppermute | solution.py:562
  55.9 9.5 %collective-permute-start.12 = (bf16[80,768]{1,0:T(8,128)(2,1)S(1)}, bf16[80,768]{1,0:T(8,128)(2,1)S(1)}, u32[]{:S(2)}, u32[]{:S(2)}) collective-permute-start(bf16[80,768]{1,0:T(8,128)(2,1)S(1)} %collective-permute-done.11.refs_2_), channel_id=1, source_target_pairs={{0,16},{16,0},{1,17},{17,1},{2,18},{18,2},{3,19},{19,3},{4,20},{20... | collective-permute-start | bytes 368648 | tf_op jit(solution)/shard_map/ppermute | solution.py:562
  56.4 9.0 %collective-permute-start.14 = (bf16[80,768]{1,0:T(8,128)(2,1)S(1)}, bf16[80,768]{1,0:T(8,128)(2,1)S(1)}, u32[]{:S(2)}, u32[]{:S(2)}) collective-permute-start(bf16[80,768]{1,0:T(8,128)(2,1)S(1)} %collective-permute-done.13.refs_4_), channel_id=1, source_target_pairs={{0,16},{16,0},{1,17},{17,1},{2,18},{18,2},{3,19},{19,3},{4,20},{20... | collective-permute-start | bytes 368648 | tf_op jit(solution)/shard_map/ppermute | solution.py:562
  56.5 8.9 %collective-permute-start.16 = (bf16[80,768]{1,0:T(8,128)(2,1)}, bf16[80,768]{1,0:T(8,128)(2,1)S(1)}, u32[]{:S(2)}, u32[]{:S(2)}) collective-permute-start(bf16[80,768]{1,0:T(8,128)(2,1)} %collective-permute-done.15.refs_6_), channel_id=1, source_target_pairs={{0,16},{16,0},{1,17},{17,1},{2,18},{18,2},{3,19},{19,3},{4,20},{20... | collective-permute-start | bytes 368648 | tf_op jit(solution)/shard_map/ppermute | solution.py:562
  64.4 19.6 %collective-permute-start.17 = (bf16[512,128]{1,0:T(8,128)(2,1)S(1)}, bf16[512,128]{1,0:T(8,128)(2,1)S(1)}, u32[]{:S(2)}, u32[]{:S(2)}) collective-permute-start(bf16[512,128]{1,0:T(8,128)(2,1)S(1)} %get-tuple-element.81.refs_1_), channel_id=1, source_target_pairs={{0,1},{1,0},{2,3},{3,2},{4,5},{5,4},{6,7},{7,6},{8,9},{9,8},{10,11... | collective-permute-start | bytes 393224 | tf_op jit(solution)/shard_map/ppermute | solution.py:571
  66.5 32.5 %collective-permute-start.19 = (bf16[512,128]{1,0:T(8,128)(2,1)S(1)}, bf16[512,128]{1,0:T(8,128)(2,1)S(1)}, u32[]{:S(2)}, u32[]{:S(2)}) collective-permute-start(bf16[512,128]{1,0:T(8,128)(2,1)S(1)} %get-tuple-element.81.refs_1_), channel_id=1, source_target_pairs={{0,2},{1,3},{2,0},{3,1},{4,6},{5,7},{6,4},{7,5},{8,10},{9,11},{10,... | collective-permute-start | bytes 393224 | tf_op jit(solution)/shard_map/ppermute | solution.py:571
  68.1 45.9 %collective-permute-start.21 = (bf16[512,128]{1,0:T(8,128)(2,1)S(1)}, bf16[512,128]{1,0:T(8,128)(2,1)S(1)}, u32[]{:S(2)}, u32[]{:S(2)}) collective-permute-start(bf16[512,128]{1,0:T(8,128)(2,1)S(1)} %get-tuple-element.81.refs_1_), channel_id=1, source_target_pairs={{0,3},{1,2},{2,1},{3,0},{4,7},{5,6},{6,5},{7,4},{8,11},{9,10},{10,... | collective-permute-start | bytes 393224 | tf_op jit(solution)/shard_map/ppermute | solution.py:571
  113.9 29.2 %copy-start.4 = (s32[512,1]{1,0:T(8,128)S(1)}, s32[512,1]{1,0:T(8,128)}, u32[]{:S(2)}) copy-start(s32[512,1]{1,0:T(8,128)} %copy-done.3) | copy-start | bytes 6148
  113.9 29.2 %copy-start.7 = (f32[290,128]{1,0:T(8,128)S(1)}, f32[290,128]{1,0:T(8,128)}, u32[]{:S(2)}) copy-start(f32[290,128]{1,0:T(8,128)} %refs_3_.6) | copy-start | bytes 445444
  128.9 34.9 %copy-start.19 = (f32[768,64]{0,1:T(8,128)S(1)}, f32[768,64]{0,1:T(8,128)}, u32[]{:S(2)}) copy-start(f32[768,64]{0,1:T(8,128)} %param.25) | copy-start | bytes 589828
  128.9 75.1 %copy-start.1 = (f32[64,768]{1,0:T(8,128)S(1)}, f32[64,768]{1,0:T(8,128)}, u32[]{:S(2)}) copy-start(f32[64,768]{1,0:T(8,128)} %refs_8_.2) | copy-start | bytes 589828
  128.9 75.1 %copy-start.15 = (f32[1,768]{1,0:T(1,128)S(1)}, f32[1,768]{1,0:T(1,128)}, u32[]{:S(2)}) copy-start(f32[1,768]{1,0:T(1,128)} %refs_10_.1) | copy-start | bytes 9220
  128.9 75.1 %copy-start.16 = (f32[1,768]{1,0:T(1,128)S(1)}, f32[1,768]{1,0:T(1,128)}, u32[]{:S(2)}) copy-start(f32[1,768]{1,0:T(1,128)} %refs_5_.3) | copy-start | bytes 9220
  128.9 75.1 %copy-start.17 = (f32[1,768]{1,0:T(1,128)S(1)}, f32[1,768]{1,0:T(1,128)}, u32[]{:S(2)}) copy-start(f32[1,768]{1,0:T(1,128)} %refs_6_.3) | copy-start | bytes 9220
  129.0 10.3 %collective-permute-start.22 = (f32[512,128]{1,0:T(8,128)S(1)}, f32[512,128]{1,0:T(8,128)S(1)}, u32[]{:S(2)}, u32[]{:S(2)}) collective-permute-start(f32[512,128]{1,0:T(8,128)S(1)} %get-tuple-element.95), channel_id=1, source_target_pairs={{0,3},{1,2},{2,1},{3,0},{4,7},{5,6},{6,5},{7,4},{8,11},{9,10},{10,... | collective-permute-start | bytes 786440 | tf_op jit(solution)/shard_map/ppermute | solution.py:571
  130.9 12.1 %collective-permute-start.20 = (f32[512,128]{1,0:T(8,128)S(1)}, f32[512,128]{1,0:T(8,128)S(1)}, u32[]{:S(2)}, u32[]{:S(2)}) collective-permute-start(f32[512,128]{1,0:T(8,128)S(1)} %get-tuple-element.92), channel_id=1, source_target_pairs={{0,2},{1,3},{2,0},{3,1},{4,6},{5,7},{6,4},{7,5},{8,10},{9,11},{10,... | collective-permute-start | bytes 786440 | tf_op jit(solution)/shard_map/ppermute | solution.py:571
  131.4 11.7 %collective-permute-start.18 = (f32[512,128]{1,0:T(8,128)S(1)}, f32[512,128]{1,0:T(8,128)S(1)}, u32[]{:S(2)}, u32[]{:S(2)}) collective-permute-start(f32[512,128]{1,0:T(8,128)S(1)} %get-tuple-element.89), channel_id=1, source_target_pairs={{0,1},{1,0},{2,3},{3,2},{4,5},{5,4},{6,7},{7,6},{8,9},{9,8},{10,11... | collective-permute-start | bytes 786440 | tf_op jit(solution)/shard_map/ppermute | solution.py:571
  147.0 15.9 %copy-start.18 = (f32[160,128]{1,0:T(8,128)}, f32[160,128]{1,0:T(8,128)S(1)}, u32[]{:S(2)}) copy-start(f32[160,128]{1,0:T(8,128)S(1)} %get-tuple-element.97) | copy-start | bytes 245764
  147.0 6.4 %collective-permute-start.31 = (bf16[512,128]{1,0:T(8,128)(2,1)S(1)}, bf16[512,128]{1,0:T(8,128)(2,1)S(1)}, u32[]{:S(2)}, u32[]{:S(2)}) collective-permute-start(bf16[512,128]{1,0:T(8,128)(2,1)S(1)} %get-tuple-element.99.refs_0_), channel_id=1, source_target_pairs={{0,1},{1,0},{2,3},{3,2},{4,5},{5,4},{6,7},{7,6},{8,9},{9,8},{10,11... | collective-permute-start | bytes 393224 | tf_op jit(solution)/shard_map/ppermute | solution.py:571
  148.0 7.8 %collective-permute-start.32 = (bf16[512,128]{1,0:T(8,128)(2,1)S(1)}, bf16[512,128]{1,0:T(8,128)(2,1)S(1)}, u32[]{:S(2)}, u32[]{:S(2)}) collective-permute-start(bf16[512,128]{1,0:T(8,128)(2,1)S(1)} %get-tuple-element.99.refs_0_), channel_id=1, source_target_pairs={{0,2},{1,3},{2,0},{3,1},{4,6},{5,7},{6,4},{7,5},{8,10},{9,11},{10,... | collective-permute-start | bytes 393224 | tf_op jit(solution)/shard_map/ppermute | solution.py:571
  149.2 6.6 %collective-permute-start.33 = (bf16[512,128]{1,0:T(8,128)(2,1)S(1)}, bf16[512,128]{1,0:T(8,128)(2,1)S(1)}, u32[]{:S(2)}, u32[]{:S(2)}) collective-permute-start(bf16[512,128]{1,0:T(8,128)(2,1)S(1)} %get-tuple-element.99.refs_0_), channel_id=1, source_target_pairs={{0,3},{1,2},{2,1},{3,0},{4,7},{5,6},{6,5},{7,4},{8,11},{9,10},{10,... | collective-permute-start | bytes 393224 | tf_op jit(solution)/shard_map/ppermute | solution.py:571
  150.5 22.3 %collective-permute-start.38 = (f32[4,72,768]{2,1,0:T(8,128)S(1)}, f32[4,72,768]{2,1,0:T(8,128)}, u32[]{:S(2)}, u32[]{:S(2)}) collective-permute-start(f32[4,72,768]{2,1,0:T(8,128)S(1)} %get-tuple-element.104), channel_id=1, source_target_pairs={{0,16},{16,0},{1,17},{17,1},{2,18},{18,2},{3,19},{19,3},{4,20},{20... | collective-permute-start | bytes 2654216 | tf_op jit(solution)/shard_map/ppermute | solution.py:562
  163.8 11.6 %collective-permute-start.34 = (f32[4,64,768]{2,1,0:T(8,128)}, f32[4,64,768]{2,1,0:T(8,128)}, u32[]{:S(2)}, u32[]{:S(2)}) collective-permute-start(f32[4,64,768]{2,1,0:T(8,128)} %get-tuple-element.101), channel_id=1, source_target_pairs={{0,16},{16,0},{1,17},{17,1},{2,18},{18,2},{3,19},{19,3},{4,20},{20... | collective-permute-start | bytes 2359304 | tf_op jit(solution)/shard_map/ppermute | solution.py:562
  166.9 1.7 collective-permute-start.23
  168.6 9.7 %collective-permute-start.24 = (f32[160,128]{1,0:T(8,128)S(1)}, f32[160,128]{1,0:T(8,128)S(1)}, u32[]{:S(2)}, u32[]{:S(2)}) collective-permute-start(f32[160,128]{1,0:T(8,128)S(1)} %add.174), channel_id=1, source_target_pairs={{0,12},{4,0},{8,4},{12,8},{1,13},{5,1},{9,5},{13,9},{2,14},{6,2},{... | collective-permute-start | bytes 245768 | tf_op jit(solution)/shard_map/ppermute | solution.py:565
  170.4 19.0 %collective-permute-start.25 = (f32[160,128]{1,0:T(8,128)S(1)}, f32[160,128]{1,0:T(8,128)S(1)}, u32[]{:S(2)}, u32[]{:S(2)}) collective-permute-start(f32[160,128]{1,0:T(8,128)S(1)} %add.174), channel_id=1, source_target_pairs={{0,8},{4,12},{8,0},{12,4},{1,9},{5,13},{9,1},{13,5},{2,10},{6,14},... | collective-permute-start | bytes 245768 | tf_op jit(solution)/shard_map/ppermute | solution.py:565
  170.9 18.5 %collective-permute-start.26 = (f32[160,128]{1,0:T(8,128)S(1)}, f32[160,128]{1,0:T(8,128)S(1)}, u32[]{:S(2)}, u32[]{:S(2)}) collective-permute-start(f32[160,128]{1,0:T(8,128)S(1)} %add.174), channel_id=1, source_target_pairs={{0,4},{4,8},{8,12},{12,0},{1,5},{5,9},{9,13},{13,1},{2,6},{6,10},{... | collective-permute-start | bytes 245768 | tf_op jit(solution)/shard_map/ppermute | solution.py:565
  174.2 15.2 %collective-permute-start.39 = (f32[72,768]{1,0:T(8,128)S(1)}, f32[72,768]{1,0:T(8,128)S(1)}, u32[]{:S(2)}, u32[]{:S(2)}) collective-permute-start(f32[72,768]{1,0:T(8,128)S(1)} %get-tuple-element.173), channel_id=1, source_target_pairs={{0,4},{4,8},{8,12},{12,0},{1,5},{5,9},{9,13},{13,1},{2,6},{6,10},{... | collective-permute-start | bytes 663560 | tf_op jit(solution)/shard_map/ppermute | solution.py:568
  175.3 26.5 %collective-permute-start.40 = (f32[72,768]{1,0:T(8,128)S(1)}, f32[72,768]{1,0:T(8,128)S(1)}, u32[]{:S(2)}, u32[]{:S(2)}) collective-permute-start(f32[72,768]{1,0:T(8,128)S(1)} %get-tuple-element.172), channel_id=1, source_target_pairs={{0,8},{4,12},{8,0},{12,4},{1,9},{5,13},{9,1},{13,5},{2,10},{6,14},... | collective-permute-start | bytes 663560 | tf_op jit(solution)/shard_map/ppermute | solution.py:568
  178.3 24.8 %collective-permute-start.41 = (f32[72,768]{1,0:T(8,128)S(1)}, f32[72,768]{1,0:T(8,128)S(1)}, u32[]{:S(2)}, u32[]{:S(2)}) collective-permute-start(f32[72,768]{1,0:T(8,128)S(1)} %get-tuple-element.171), channel_id=1, source_target_pairs={{0,12},{4,0},{8,4},{12,8},{1,13},{5,1},{9,5},{13,9},{2,14},{6,2},{... | collective-permute-start | bytes 663560 | tf_op jit(solution)/shard_map/ppermute | solution.py:568
  189.4 17.4 %collective-permute-start.35 = (f32[64,768]{1,0:T(8,128)S(1)}, f32[64,768]{1,0:T(8,128)S(1)}, u32[]{:S(2)}, u32[]{:S(2)}) collective-permute-start(f32[64,768]{1,0:T(8,128)S(1)} %get-tuple-element.176), channel_id=1, source_target_pairs={{0,4},{4,8},{8,12},{12,0},{1,5},{5,9},{9,13},{13,1},{2,6},{6,10},{... | collective-permute-start | bytes 589832 | tf_op jit(solution)/shard_map/ppermute | solution.py:568
  189.4 22.1 %collective-permute-start.36 = (f32[64,768]{1,0:T(8,128)S(1)}, f32[64,768]{1,0:T(8,128)S(1)}, u32[]{:S(2)}, u32[]{:S(2)}) collective-permute-start(f32[64,768]{1,0:T(8,128)S(1)} %get-tuple-element.175), channel_id=1, source_target_pairs={{0,8},{4,12},{8,0},{12,4},{1,9},{5,13},{9,1},{13,5},{2,10},{6,14},... | collective-permute-start | bytes 589832 | tf_op jit(solution)/shard_map/ppermute | solution.py:568
  189.4 22.1 %collective-permute-start.37 = (f32[64,768]{1,0:T(8,128)S(1)}, f32[64,768]{1,0:T(8,128)S(1)}, u32[]{:S(2)}, u32[]{:S(2)}) collective-permute-start(f32[64,768]{1,0:T(8,128)S(1)} %get-tuple-element.174), channel_id=1, source_target_pairs={{0,12},{4,0},{8,4},{12,8},{1,13},{5,1},{9,5},{13,9},{2,14},{6,2},{... | collective-permute-start | bytes 589832 | tf_op jit(solution)/shard_map/ppermute | solution.py:568
  201.9 15.3 %collective-permute-start.27 = (f32[160,128]{1,0:T(8,128)S(1)}, f32[160,128]{1,0:T(8,128)S(1)}, u32[]{:S(2)}, u32[]{:S(2)}) collective-permute-start(f32[160,128]{1,0:T(8,128)S(1)} %add_add_fusion.1), channel_id=1, source_target_pairs={{0,1},{1,0},{2,3},{3,2},{4,5},{5,4},{6,7},{7,6},{8,9},{9,8},{10,11... | collective-permute-start | bytes 245768 | tf_op jit(solution)/shard_map/ppermute | solution.py:571
  203.1 15.3 %collective-permute-start.28 = (f32[160,128]{1,0:T(8,128)S(1)}, f32[160,128]{1,0:T(8,128)S(1)}, u32[]{:S(2)}, u32[]{:S(2)}) collective-permute-start(f32[160,128]{1,0:T(8,128)S(1)} %add_add_fusion.1), channel_id=1, source_target_pairs={{0,2},{1,3},{2,0},{3,1},{4,6},{5,7},{6,4},{7,5},{8,10},{9,11},{10,... | collective-permute-start | bytes 245768 | tf_op jit(solution)/shard_map/ppermute | solution.py:571
  204.0 0.9 copy-start.9
  206.8 21.4 %copy-start.11 = (f32[64,768]{1,0:T(8,128)}, f32[64,768]{1,0:T(8,128)S(1)}, u32[]{:S(2)}) copy-start(f32[64,768]{1,0:T(8,128)S(1)} %get-tuple-element.112.refs_9_) | copy-start | bytes 589828
  206.8 11.7 %collective-permute-start.29 = (f32[160,128]{1,0:T(8,128)S(1)}, f32[160,128]{1,0:T(8,128)S(1)}, u32[]{:S(2)}, u32[]{:S(2)}) collective-permute-start(f32[160,128]{1,0:T(8,128)S(1)} %add_add_fusion.1), channel_id=1, source_target_pairs={{0,3},{1,2},{2,1},{3,0},{4,7},{5,6},{6,5},{7,4},{8,11},{9,10},{10,... | collective-permute-start | bytes 245768 | tf_op jit(solution)/shard_map/ppermute | solution.py:571
  211.5 1.0 copy-start.2
  213.8 1.2 collective-permute-start.42
  215.0 3.6 %collective-permute-start.43 = (f32[8,128]{1,0:T(8,128)S(1)}, f32[8,128]{1,0:T(8,128)S(1)}, u32[]{:S(2)}, u32[]{:S(2)}) collective-permute-start(f32[8,128]{1,0:T(8,128)S(1)} %add.199), channel_id=1, source_target_pairs={{0,1},{1,0},{2,3},{3,2},{4,5},{5,4},{6,7},{7,6},{8,9},{9,8},{10,11... | collective-permute-start | bytes 12296 | tf_op jit(solution)/shard_map/ppermute | solution.py:571
  216.2 3.6 %collective-permute-start.44 = (f32[8,128]{1,0:T(8,128)S(1)}, f32[8,128]{1,0:T(8,128)S(1)}, u32[]{:S(2)}, u32[]{:S(2)}) collective-permute-start(f32[8,128]{1,0:T(8,128)S(1)} %add.199), channel_id=1, source_target_pairs={{0,2},{1,3},{2,0},{3,1},{4,6},{5,7},{6,4},{7,5},{8,10},{9,11},{10,... | collective-permute-start | bytes 12296 | tf_op jit(solution)/shard_map/ppermute | solution.py:571
  217.1 4.5 %collective-permute-start.45 = (f32[8,128]{1,0:T(8,128)S(1)}, f32[8,128]{1,0:T(8,128)S(1)}, u32[]{:S(2)}, u32[]{:S(2)}) collective-permute-start(f32[8,128]{1,0:T(8,128)S(1)} %add.199), channel_id=1, source_target_pairs={{0,3},{1,2},{2,1},{3,0},{4,7},{5,6},{6,5},{7,4},{8,11},{9,10},{10,... | collective-permute-start | bytes 12296 | tf_op jit(solution)/shard_map/ppermute | solution.py:571
  218.5 12.0 %collective-permute-start.30 = (f32[160,128]{1,0:T(8,128)S(1)}, f32[160,128]{1,0:T(8,128)S(1)}, u32[]{:S(2)}, u32[]{:S(2)}) collective-permute-start(f32[160,128]{1,0:T(8,128)S(1)} %add_add_fusion.refs_1_), channel_id=1, source_target_pairs={{0,16},{16,0},{1,17},{17,1},{2,18},{18,2},{3,19},{19,3},{4,20},{20... | collective-permute-start | bytes 245768 | tf_op jit(solution)/shard_map/ppermute | solution.py:562
  221.6 16.4 %collective-permute-start.46 = (f32[8,128]{1,0:T(8,128)S(1)}, f32[8,128]{1,0:T(8,128)S(1)}, u32[]{:S(2)}, u32[]{:S(2)}) collective-permute-start(f32[8,128]{1,0:T(8,128)S(1)} %add_add_fusion.2.refs_2_), channel_id=1, source_target_pairs={{0,12},{4,0},{8,4},{12,8},{1,13},{5,1},{9,5},{13,9},{2,14},{6,2},{... | collective-permute-start | bytes 12296 | tf_op jit(solution)/shard_map/ppermute | solution.py:565
  228.2 9.9 %collective-permute-start.47 = (f32[8,128]{1,0:T(8,128)S(1)}, f32[8,128]{1,0:T(8,128)S(1)}, u32[]{:S(2)}, u32[]{:S(2)}) collective-permute-start(f32[8,128]{1,0:T(8,128)S(1)} %add_add_fusion.2.refs_2_), channel_id=1, source_target_pairs={{0,8},{4,12},{8,0},{12,4},{1,9},{5,13},{9,1},{13,5},{2,10},{6,14},... | collective-permute-start | bytes 12296 | tf_op jit(solution)/shard_map/ppermute | solution.py:565
  228.2 9.9 %collective-permute-start.48 = (f32[8,128]{1,0:T(8,128)S(1)}, f32[8,128]{1,0:T(8,128)S(1)}, u32[]{:S(2)}, u32[]{:S(2)}) collective-permute-start(f32[8,128]{1,0:T(8,128)S(1)} %add_add_fusion.2.refs_2_), channel_id=1, source_target_pairs={{0,4},{4,8},{8,12},{12,0},{1,5},{5,9},{9,13},{13,1},{2,6},{6,10},{... | collective-permute-start | bytes 12296 | tf_op jit(solution)/shard_map/ppermute | solution.py:565
  238.0 0.9 copy-start.12
  (5 other events, 4.6 us)
